TPU v7x, 128 devices: a whole 4x4x4 slice. The times are simulated.
128 devices in a mesh: batch: 2 (over core), ctx: 64 (over x, y, z).
Axes of the slice: x: 4, y: 4, z: 4, core: 2. Of those that a mesh axis runs over, the one named last changes fastest.
Arguments:
- tokens: int32 [4, 16384], P('batch', 'ctx'), parts along dimension 0, may hold values from 65 to 116, as said below
- lengths: int32 [4], P('batch'), parts along dimension 0, may hold values from 4096 to 16384, as said below
- feature_table: bfloat16 [512, 12288], replicated, may hold values from -6 to 6
- short_filter: float32 [3, 12288], replicated, may hold values from -3 to 3
- long_filter: bfloat16 [256, 128], replicated, may hold values from -0.5 to 0.5
- queries: bfloat16 [64, 4096], replicated, may hold values from -210 to 210
Outputs:
- mixer_field: bfloat16 [4, 16384, 4096], P('batch', 'ctx'), parts along dimension 0
- pooled: float32 [4, 64, 4096], P('batch'), parts along dimension 0
There are 2 independent parts, one for each index of `batch`. A program takes and returns all parts, laid end to end along the dimension named above; an argument that names none is the same for every part. Nothing has to cross between parts.
Inputs may be any that keep to these rules, and one draw needn't show every extreme that they name: `tokens`: every token is the byte code of one of the bases A, C, G, T in upper or lower case. `lengths`: in every part at least one window has all 16384 positions valid.
All inputs are finite; a program needn't handle non-finite values.
Results may differ from a plain program's by a relative error of at most 0.0065.
The roundings to bfloat16 on the way count: a program that leaves them out, or rounds other values in their place, can miss the bound.
Values may be sent and summed in bfloat16 or wider, within the bound.
A program may use at most 192 MiB of HBM per device.

v0:
```python
import jax
import jax.numpy as jnp
from jax import lax
from jax.sharding import PartitionSpec as P


def passed_along(value, axis, steps):
    count = lax.axis_size(axis)
    leading, last = (max(0, -steps), min(count, count - steps))
    return lax.ppermute(value, axis, [(source, source + steps) for source in range(leading, last)])


def short_pass(source, short_filter):
    count = source.shape[1] - 2
    return (
        short_filter[0] * source[:, 2:]
        + short_filter[1] * source[:, 1 : count + 1]
        + short_filter[2] * source[:, :count]
    )


def kernel_rows(long_filter):
    tap_count = long_filter.shape[1]
    out_pos = jnp.arange(tap_count)[:, None]
    in_pos = jnp.arange(2 * tap_count)[None, :]
    offset = out_pos + tap_count - in_pos
    usable = (offset >= 0) & (offset < tap_count)
    picked = jnp.take(long_filter, jnp.clip(offset, 0, tap_count - 1), axis=1)
    return jnp.where(usable[None], picked, jnp.zeros_like(picked))


def long_pass(extended, long_filter):
    windows, total, model_width = extended.shape
    tap_count = long_filter.shape[1]
    group_count = long_filter.shape[0]
    group_width = model_width // group_count
    row_count = total - tap_count
    block_count = row_count // tap_count
    kernel = kernel_rows(long_filter)
    previous = extended[:, :row_count].reshape(
        windows, block_count, tap_count, group_count, group_width
    )
    current = extended[:, tap_count:].reshape(
        windows, block_count, tap_count, group_count, group_width
    )
    result = jnp.einsum(
        "gim,wbmgc->wbigc", kernel[:, :, :tap_count], previous, preferred_element_type=jnp.float32
    )
    result = result + jnp.einsum(
        "gim,wbmgc->wbigc", kernel[:, :, tap_count:], current, preferred_element_type=jnp.float32
    )
    return result.reshape(windows, row_count, model_width)


def on_device(tokens, lengths, feature_table, short_filter, long_filter, queries):
    windows, row_count = tokens.shape
    model_width = queries.shape[1]
    tap_count = long_filter.shape[1]
    features = jnp.take(feature_table, tokens, axis=0)
    edge_rows = passed_along(features[:, row_count - 2 :], "ctx", 1)
    featurized = short_pass(jnp.concatenate([edge_rows, features], axis=1), short_filter)
    gated = (
        featurized[:, :, model_width : 2 * model_width] * featurized[:, :, 2 * model_width :]
    ).astype(jnp.bfloat16)
    carried = passed_along(gated[:, row_count - (tap_count - 1) :], "ctx", 1)
    extended = jnp.concatenate(
        [jnp.zeros((windows, 1, model_width), jnp.bfloat16), carried, gated], axis=1
    )
    convolved = long_pass(extended, long_filter)
    mixer_field = (featurized[:, :, :model_width] * convolved).astype(jnp.bfloat16)
    scores = jnp.einsum(
        "nc,wtc->wnt", queries, mixer_field, preferred_element_type=jnp.float32
    ) * model_width ** (-0.5)
    position = lax.axis_index("ctx") * row_count + jnp.arange(row_count)
    is_valid = (position[None, :] < lengths[:, None])[:, None, :]
    local_top = jnp.max(jnp.where(is_valid, scores, -jnp.inf), axis=2)
    row_top = lax.pmax(local_top, "ctx")
    shifted = jnp.where(is_valid, scores - row_top[:, :, None], 0.0)
    weights = jnp.where(is_valid, jnp.exp(shifted), 0.0).astype(jnp.bfloat16)
    weighted = jnp.einsum("wnt,wtc->wnc", weights, mixer_field, preferred_element_type=jnp.float32)
    summed = lax.psum(weighted, "ctx")
    pooled = summed / jnp.sqrt(jnp.mean(summed * summed, axis=2, keepdims=True) + 1e-06)
    return (mixer_field, pooled)


def solution(mesh):
    return jax.shard_map(
        on_device,
        mesh=mesh,
        in_specs=(P("batch", "ctx"), P("batch"), P(), P(), P(), P()),
        out_specs=(P("batch", "ctx", None), P("batch", None, None)),
        check_vma=False,
    )
```

profile of v0, /device:TPU:0, one launch (start us, length us, event | category | flops | bytes accessed | tf_op | source)
XLA Modules:
  0.0 718.5 jit_solution(10457450220528873983)
XLA Ops:
  7.2 0.0 copy-start
  7.2 0.0 all-reduce.2.cloned.1.call-start
  7.2 0.7 fusion.21
  8.0 0.7 compare_and_fusion
  8.7 28.6 %gather_fusion = bf16[512,12288]{1,0:T(8,128)(2,1)} fusion(bf16[512,12288]{1,0:T(8,128)(2,1)} %param.8, s32[1024]{0:T(1024)S(1)} %pad_clamp_fusion), kind=kCustom, calls=%fused_computation | custom fusion | bytes 25167872 | tf_op jit(solution)/shard_map/jit(_take)/gather | solution.py:59
  37.2 16.0 %copy.20 = bf16[2,256,12288]{1,2,0:T(8,128)(2,1)} copy(bf16[2,256,12288]{2,1,0:T(8,128)(2,1)} %bitcast.43) | data formatting | bytes 25165824 | tf_op jit(solution)/shard_map/jit(_take)/gather | solution.py:59
  53.2 6.7 broadcast_select_fusion
  60.0 4.5 copy-done.1
  64.5 3.9 slice.56
  68.4 5.3 copy.21
  73.7 4.1 collective-permute-start
  77.9 0.1 fusion.10
  78.0 0.2 fusion.15
  78.1 0.1 copy.39
  78.2 0.1 fusion.23
  78.4 0.1 broadcast_compare_fusion
  78.5 0.1 copy.25
  78.6 129.4 %gather_fusion.1 = bf16[32768,256]{1,0:T(8,128)(2,1)} fusion(bf16[256,128]{0,1:T(8,128)(2,1)S(1)} %copy.25, s32[32768]{0:T(1024)S(1)} %broadcast_clamp_fusion), kind=kCustom, calls=%fused_computation.1 | custom fusion | bytes 33685504 | tf_op jit(solution)/shard_map/jit(_take)/gather | solution.py:28
  208.0 23.4 %copy.37 = bf16[128,256,256]{1,0,2:T(8,128)(2,1)} copy(bf16[128,256,256]{2,1,0:T(8,128)(2,1)} %bitcast.42) | data formatting | bytes 33554432 | tf_op jit(solution)/shard_map/jit(_take)/gather | solution.py:28
  231.3 0.0 collective-permute-done
  231.4 4.7 copy.22
  236.1 32.2 %multiply_add_fusion = f32[2,256,12288]{1,2,0:T(8,128)} fusion(bf16[2,256,12288]{1,2,0:T(8,128)(2,1)} %copy-done.1, bf16[2,2,12288]{1,2,0:T(8,128)(2,1)} %copy.22, f32[12288]{0:T(1024)S(1)} %bitcast.46, f32[12288]{0:T(1024)S(1)} %bitcast.47, f32[12288]{0:T(1024)S(1)} %bitcast.45), kind=kLoop, calls=%fused_computation.2 | loop fusion | flops 88080384 | bytes 37994496 | tf_op jit(solution)/shard_map/add | solution.py:16
  268.3 6.3 fusion.3
  274.6 0.0 copy-start.3
  274.6 2.0 copy-done.3
  276.6 0.6 slice.62
  277.3 3.9 copy.23
  281.2 5.1 collective-permute-start.1
  286.3 14.3 %select_bitcast_fusion = bf16[256,128,256]{2,1,0:T(8,128)(2,1)} fusion(bf16[128,256,256]{1,0,2:T(8,128)(2,1)} %copy.37, pred[128,256]{1,0:T(8,128)(4,1)S(1)} %get-tuple-element.10, pred[128,256]{1,0:T(8,128)(4,1)S(1)} %get-tuple-element.9), kind=kLoop, calls=%fused_computation.5 | loop fusion | flops 16777216 | bytes 33619968 | tf_op jit(solution)/shard_map/jit(_where)/select_n | solution.py:29
  300.6 6.9 reshape.145
  307.5 13.7 %fusion.1 = f32[256,2,2,16,128]{4,3,2,1,0:T(8,128)} fusion(bf16[256,128,256]{2,1,0:T(8,128)(2,1)} %select_bitcast_fusion, bf16[2,2,128,256,16]{2,1,4,3,0:T(2,128)(2,1)} %reshape.145), kind=kOutput, calls=%fused_computation.10 | convolution fusion | flops 536870912 | bytes 20971520 | tf_op jit(solution)/shard_map/gim,wbmgc->wbigc/dot_general | solution.py:49
  321.2 8.3 %collective-permute-done.1 = bf16[2,127,4096]{2,0,1:T(2,128)(2,1)} collective-permute-done((bf16[2,127,4096]{2,0,1:T(2,128)(2,1)}, bf16[2,127,4096]{2,0,1:T(2,128)(2,1)}, u32[]{:S(2)}, u32[]{:S(2)}) %collective-permute-start.1) | collective-permute-done | bytes 2080800 | tf_op jit(solution)/shard_map/ppermute | solution.py:10
  329.6 5.1 copy.24
  334.7 4.4 pad_maximum_fusion.1
  339.1 6.9 reshape.144
  346.0 16.1 %add_bitcast_fusion = f32[2,2,128,256,16]{2,4,1,0,3:T(8,128)} fusion(f32[256,2,2,16,128]{4,3,2,1,0:T(8,128)} %fusion.1, bf16[256,128,256]{2,1,0:T(8,128)(2,1)} %select_bitcast_fusion, bf16[2,2,128,256,16]{2,1,4,3,0:T(2,128)(2,1)} %reshape.144), kind=kOutput, calls=%fused_computation.17 | convolution fusion | flops 538968064 | bytes 29360128 | tf_op jit(solution)/shard_map/gim,wbmgc->wbigc/dot_general | solution.py:46
  362.1 13.2 %copy.29 = f32[2,2,128,256,16]{2,1,4,3,0:T(2,128)} copy(f32[2,2,128,256,16]{2,4,1,0,3:T(8,128)} %add_bitcast_fusion) | data formatting | bytes 16777216 | tf_op jit(solution)/shard_map/add | solution.py:49
  375.3 11.5 %reshape.146 = f32[2,256,4096]{1,2,0:T(8,128)} reshape(f32[2,2,128,256,16]{2,1,4,3,0:T(2,128)} %copy.29) | data formatting | bytes 16777216 | tf_op jit(solution)/shard_map/reshape | solution.py:52
  386.8 6.7 fusion.4
  393.5 1.9 copy-done.2
  395.5 0.9 select_reduce_fusion
  396.4 179.3 %pmax.7 = f32[2,64]{1,0:T(2,128)S(1)} all-reduce(f32[2,64]{1,0:T(2,128)S(1)} %get-tuple-element.11), channel_id=1, replica_groups=mesh['batch'=2,'ctx'=64] {'ctx'}, use_global_device_ids=true, to_apply=%region_1.2 | all-reduce | flops 128 | bytes 1024 | tf_op jit(solution)/shard_map/pmax | solution.py:77
  575.7 4.9 fusion.17
  580.6 0.0 all-reduce.2.cloned.1.call-update
  580.7 6.4 copy.32
  587.0 119.6 %all-reduce.2.cloned.1.call-done = f32[2,64,4096]{2,1,0:T(8,128)} async-done(((f32[2,64,4096]{2,1,0:T(8,128)}), f32[2,64,4096]{2,1,0:T(8,128)}) %all-reduce.2.cloned.1.call-update) | async-done | bytes 2097168 | tf_op jit(solution)/shard_map/psum | solution.py:81
  706.7 1.8 multiply_reduce_fusion
  708.5 3.2 broadcast_divide_fusion
  (20 shorter events, 0.1 us)
Async XLA Ops:
  7.2 388.3 %copy-start = (bf16[64,4096]{1,0:T(8,128)(2,1)S(1)}, bf16[64,4096]{1,0:T(8,128)(2,1)}, u32[]{:S(2)}) copy-start(bf16[64,4096]{1,0:T(8,128)(2,1)} %param.11) | copy-start | bytes 1572868
  7.2 699.5 %all-reduce.2.cloned.1.call-start = ((), (), s32[]{:S(2)}) async-start(), calls=%async_computation | async-start | bytes 4194304 | tf_op jit(solution)/shard_map/psum | solution.py:81
  59.9 4.5 copy-start.1
  64.5 13.7 %copy-start.4 = (f32[3,12288]{1,0:T(4,128)S(1)}, f32[3,12288]{1,0:T(4,128)}, u32[]{:S(2)}) copy-start(f32[3,12288]{1,0:T(4,128)} %param.9) | copy-start | bytes 442372
  64.5 13.9 %copy-start.7 = (s32[2]{0:T(128)S(1)}, s32[2]{0:T(128)}, u32[]{:S(2)}) copy-start(s32[2]{0:T(128)} %param.7) | copy-start | bytes 28
  64.5 14.0 %copy-start.5 = (bf16[256,128]{1,0:T(8,128)(2,1)S(1)}, bf16[256,128]{1,0:T(8,128)(2,1)}, u32[]{:S(2)}) copy-start(bf16[256,128]{1,0:T(8,128)(2,1)} %param.10) | copy-start | bytes 196612
  73.7 157.6 %collective-permute-start = (bf16[2,2,12288]{2,1,0:T(2,128)(2,1)S(1)}, bf16[2,2,12288]{2,1,0:T(2,128)(2,1)S(1)}, u32[]{:S(2)}, u32[]{:S(2)}) collective-permute-start(bf16[2,2,12288]{2,1,0:T(2,128)(2,1)S(1)} %copy.21), channel_id=1, source_target_pairs={{0,1},{1,2},{2,3},{3,4},{4,5},{5,6},{6,7},{7,8},{8,9},{9,10},{10,1... | collective-permute-start | bytes 294920 | tf_op jit(solution)/shard_map/ppermute | solution.py:10
  231.3 36.9 %copy-start.6 = (bf16[384]{0:T(512)(128)(2,1)}, bf16[384]{0:T(512)(128)(2,1)S(1)}, u32[]{:S(2)}) copy-start(bf16[384]{0:T(512)(128)(2,1)S(1)} %pad.clone) | copy-start | bytes 2308
  274.6 2.0 copy-start.3
  281.2 48.4 %collective-permute-start.1 = (bf16[2,127,4096]{2,0,1:T(2,128)(2,1)}, bf16[2,127,4096]{2,0,1:T(2,128)(2,1)}, u32[]{:S(2)}, u32[]{:S(2)}) collective-permute-start(bf16[2,127,4096]{2,0,1:T(2,128)(2,1)} %copy.23), channel_id=1, source_target_pairs={{0,1},{1,2},{2,3},{3,4},{4,5},{5,6},{6,7},{7,8},{8,9},{9,10},{10,1... | collective-permute-start | bytes 6242312 | tf_op jit(solution)/shard_map/ppermute | solution.py:10
  307.5 27.2 %slice-start = ((bf16[384]{0:T(512)(128)(2,1)}), bf16[256]{0:T(256)(128)(2,1)S(1)}, s32[]{:S(2)}) async-start(bf16[384]{0:T(512)(128)(2,1)} %copy-done.6), calls=%async_computation.1 | async-start | bytes 1024 | tf_op jit(solution)/shard_map/slice | solution.py:40
  393.5 1.9 copy-start.2
Sparse Core Ops, SparseCore 0:
  580.8 125.8 all-reduce.1
where the time goes:
time: 721 us; the launch traced here: 719 us
  local copies, waits for them, and re-layouts  275 us (38%)
  blocking collectives  179 us (25%)
  waiting for transfers between devices  128 us (18%)
  other arithmetic  77.4 us (11%)
  matrix products  35.6 us (5%)
  between operations  14.2 us (2%)
  starting transfers between devices  9.25 us (1%)
    pmax x1, blocking collectives, on_device(): row_top = lax.pmax(local_top, 'ctx')  179 us
    gather x2, local copies, waits for them, and re-layouts, kernel_rows(): picked = jnp.take(long_filter, jnp.clip(offset, 0, tap_count - 1), axis=1)  153 us
    psum x1, waiting for transfers between devices, on_device(): summed = lax.psum(weighted, 'ctx')  120 us
    gather x2, local copies, waits for them, and re-layouts, on_device(): features = jnp.take(feature_table, tokens, axis=0)  44.6 us
    add x1, other arithmetic, short_pass(): short_filter[0] * source[:, 2:] + short_filter[1] * source[:, 1:count + 1]  32.2 us
    dot_general x1, matrix products, long_pass(): jnp.einsum('gim,wbmgc->wbigc', kernel[:, :, :tap_count], previous, prefer...  16.1 us
    unnamed x20, local copies, waits for them, and re-layouts  15 us
  transfers between devices with their start and end apart: 3, of which 2 were waited for; matrix products, arithmetic and copies ran while one was open for 27% of the time, Pallas kernels for 0%

commit v1 on v0

v1 whole, which is shorter than its diff:
```python
import functools

import jax
import jax.numpy as jnp
from jax import lax
from jax.experimental import pallas as pl
from jax.experimental.pallas import tpu as pltpu
from jax.sharding import PartitionSpec as P

bf16, f32 = jnp.bfloat16, jnp.float32
CODES = (65, 67, 71, 84, 97, 99, 103, 116)
STRIDES = (16, 4, 1)
MESH = pl.DeviceIdType.MESH
CB = 256
GPC = CB // 16
T = 128
LOWEST = -1e38


def prep_kernel(tok_ref, table_ref, sf_ref, oh_ref, tab_ref, rows_s, prev_s, load_sem, send_sem, recv_sem):
    me = lax.axis_index("ctx")
    core = lax.axis_index("batch")
    nxt, prv = lax.rem(me + 1, 64), lax.rem(me + 63, 64)
    load = pltpu.make_async_copy(table_ref.at[pl.ds(64, 64)], rows_s, load_sem)
    load.start()
    barrier = pltpu.get_barrier_semaphore()
    pl.semaphore_signal(barrier, inc=1, device_id=(core, prv), device_id_type=MESH)
    pl.semaphore_wait(barrier, 1)
    send = pltpu.make_async_remote_copy(
        src_ref=tok_ref, dst_ref=prev_s, send_sem=send_sem, recv_sem=recv_sem,
        device_id=(core, nxt), device_id_type=MESH)
    send.start()
    load.wait()
    sel_row = lax.broadcasted_iota(jnp.int32, (32, 64), 0)
    sel_col = lax.broadcasted_iota(jnp.int32, (32, 64), 1)
    want = jnp.full((32, 64), -1, jnp.int32)
    for n in range(24):
        want = jnp.where(sel_row == n, CODES[n % 8] - 64, want)
    select = jnp.where(sel_col == want, 1.0, 0.0).astype(bf16)
    e_r = lax.broadcasted_iota(jnp.int32, (T, T), 0)
    e_c = lax.broadcasted_iota(jnp.int32, (T, T), 1)
    eye = jnp.where(e_r == e_c, 1.0, 0.0).astype(bf16)

    @pl.loop(0, 48)
    def _(step):
        for u in range(2):
            cols = pl.ds(pl.multiple_of((2 * step + u) * T, T), T)
            picked = jnp.dot(select, rows_s[:, cols], preferred_element_type=f32)[:24]
            gains = jnp.concatenate([jnp.broadcast_to(sf_ref[n:n + 1, cols], (8, T)) for n in range(3)], axis=0)
            prod = picked * gains
            hi = prod.astype(bf16).astype(f32)
            rest = prod - hi
            mid = rest.astype(bf16).astype(f32)
            low = rest - mid
            stacked = jnp.concatenate([hi, mid, low, jnp.zeros((56, T), f32)], axis=0).astype(bf16)
            turned = lax.dot_general(eye, stacked, (((1,), (1,)), ((), ())), preferred_element_type=f32)
            tab_ref[cols, :] = turned.astype(bf16)

    send.wait()
    codes = jnp.zeros((8, 384), jnp.int32)
    code_row = lax.broadcasted_iota(jnp.int32, (8, 384), 0)
    for n in range(8):
        codes = jnp.where(code_row == n, CODES[n], codes)
    prev = jnp.where(me == 0, -1, prev_s[...])
    for w in range(2):
        ext = jnp.concatenate([prev[w:w + 1], tok_ref[w:w + 1]], axis=1)
        hot = [jnp.where(jnp.broadcast_to(ext[:, 128 - k:512 - k], (8, 384)) == codes, 1.0, 0.0) for k in range(3)]
        full = jnp.concatenate(hot * 3 + [jnp.zeros((8, 384), f32)], axis=0).astype(bf16)
        oh_ref[:, 128 * w:128 * w + 128] = full[:, :128]
        oh_ref[:, 256 + 256 * w:512 + 256 * w] = full[:, 128:]


def prep_call(tokens, table, short_filter):
    vmem = pl.BlockSpec(memory_space=pltpu.VMEM)
    return pl.pallas_call(
        prep_kernel,
        in_specs=[vmem, pl.BlockSpec(memory_space=pl.ANY), vmem],
        out_specs=[vmem, vmem],
        out_shape=[jax.ShapeDtypeStruct((80, 768), bf16), jax.ShapeDtypeStruct((12288, 128), bf16)],
        scratch_shapes=[pltpu.VMEM((64, 12288), bf16), pltpu.VMEM((2, 256), jnp.int32),
                        pltpu.SemaphoreType.DMA, pltpu.SemaphoreType.DMA, pltpu.SemaphoreType.DMA],
        compiler_params=pltpu.CompilerParams(collective_id=0, has_side_effects=True, vmem_limit_bytes=32 * 2**20),
    )(tokens, table, short_filter)


def main_kernel(first_ref, len_ref, oh_ref, tq_ref, tk_ref, tv_ref, h_ref, qry_ref,
                mix_ref, part_ref, m_s, s_s, g_s):
    i = pl.program_id(0)
    steps = pl.num_programs(0)
    oh = oh_ref[...]
    dot = functools.partial(jnp.dot, preferred_element_type=f32)
    k = dot(tk_ref[...][:, :80], oh)
    v = dot(tv_ref[...][:, :80], oh)
    g_s[...] = (k * v).astype(bf16)
    s_i = lax.broadcasted_iota(jnp.int32, (T, T), 0)
    t_i = lax.broadcasted_iota(jnp.int32, (T, T), 1)
    upper = t_i >= s_i
    h = h_ref[...].astype(f32)
    base = i * CB
    for j in range(GPC):
        circ = pltpu.roll(jnp.broadcast_to(h[j:j + 1], (T, T)), 0, 1, stride=1, stride_axis=0)
        toep = jnp.concatenate([jnp.where(upper, 0.0, circ), jnp.where(upper, circ, 0.0)], axis=0).astype(bf16)
        rows = pl.ds(16 * j, 16)
        q = dot(tq_ref[rows, :][:, :80], oh[:, 256:])
        blk = [g_s[rows, pl.ds(T * b, T)] for b in range(6)]
        lhs = jnp.concatenate([
            jnp.concatenate([blk[0], blk[2]], axis=1),
            jnp.concatenate([blk[2], blk[3]], axis=1),
            jnp.concatenate([blk[1], blk[4]], axis=1),
            jnp.concatenate([blk[4], blk[5]], axis=1)], axis=0)
        conv = dot(lhs, toep)
        conv = jnp.concatenate([conv[16 * b:16 * b + 16] for b in range(4)], axis=1)
        m_s[pl.ds(pl.multiple_of(base + 16 * j, 16), 16), :] = (q * conv).astype(bf16)
    m = m_s[pl.ds(pl.multiple_of(base, CB), CB), :]
    sc = dot(qry_ref[...], m)

    @pl.when(i == 0)
    def _():
        s_s[...] = sc

    @pl.when(i > 0)
    def _():
        s_s[...] += sc
    for w in range(2):
        mix_ref[w] = m[:, 256 * w:256 * w + 256].T

    @pl.when(i == steps - 1)
    def _():
        pos = lax.broadcasted_iota(jnp.int32, (64, 256), 1) + first_ref[0]
        for w in range(2):
            s = s_s[:, 256 * w:256 * w + 256] * (4096 ** -0.5)
            ok = pos < len_ref[w]
            top = jnp.max(jnp.where(ok, s, LOWEST), axis=1, keepdims=True)
            shifted = jnp.where(ok, s - top, 0.0)
            wt = jnp.where(ok, jnp.exp(shifted), 0.0).astype(bf16)
            for hb in range(2):
                for c in range(8):
                    cs = hb * 2048 + c * 256
                    r = lax.dot_general(wt, m_s[cs:cs + 256, 256 * w:256 * w + 256], (((1,), (1,)), ((), ())), preferred_element_type=f32).astype(bf16)
                    for p in range(4):
                        for u in range(2):
                            part_ref[2 * w + hb, p, 2 * c + u] = r[16 * p:16 * p + 16, 128 * u:128 * u + 128]
            hi = top.astype(bf16).astype(f32)
            mid = (top - hi).astype(bf16).astype(f32)
            lo = (top - hi - mid)
            lane = lax.broadcasted_iota(jnp.int32, (64, 128), 1)
            tile = jnp.where(lane == 0, hi, jnp.where(lane == 1, mid, jnp.where(lane == 2, lo, 0.0))).astype(bf16)
            for hb in range(2):
                for p in range(4):
                    part_ref[2 * w + hb, p, 16] = tile[16 * p:16 * p + 16]

def main_call(first, lengths, oh, tab, h, qry):
    n = 4096 // CB
    smem = pl.BlockSpec(memory_space=pltpu.SMEM)
    return pl.pallas_call(
        main_kernel, grid=(n,),
        in_specs=[smem, smem,
            pl.BlockSpec((80, 768), lambda i: (0, 0)),
            pl.BlockSpec((CB, 128), lambda i: (i, 0)),
            pl.BlockSpec((CB, 128), lambda i: (i + n, 0)),
            pl.BlockSpec((CB, 128), lambda i: (i + 2 * n, 0)),
            pl.BlockSpec((GPC, 128), lambda i: (i, 0)),
            pl.BlockSpec((64, CB), lambda i: (0, i))],
        out_specs=[pl.BlockSpec((2, 256, CB), lambda i: (0, 0, i)),
                   pl.BlockSpec((4, 4, 17, 16, 128), lambda i: (0, 0, 0, 0, 0))],
        out_shape=[jax.ShapeDtypeStruct((2, 256, 4096), bf16), jax.ShapeDtypeStruct((4, 4, 17, 16, 128), bf16)],
        scratch_shapes=[pltpu.VMEM((4096, 512), bf16), pltpu.VMEM((64, 512), f32), pltpu.VMEM((CB, 768), bf16)],
        compiler_params=pltpu.CompilerParams(vmem_limit_bytes=48 * 2**20, dimension_semantics=("arbitrary",)),
    )(first, lengths, oh, tab, tab, tab, h, qry)


def exchange_kernel(part_ref, out_ref, own_s, r1, s1f, s2, r2, s2f, s3, r3, own_sem, send_sem, recv_sem):
    me = lax.axis_index("ctx")
    core = lax.axis_index("batch")
    coord = [lax.rem(me // st, 4) for st in STRIDES]
    peer = [[me + (lax.rem(coord[a] + d, 4) - coord[a]) * STRIDES[a] for d in range(4)] for a in range(3)]

    def mixed(values, p, stage):
        first, second = values[(p + stage) % 3], values[(p + stage + 1) % 3]
        return first + core * (second - first)

    mine = [[mixed(coord, p, s) for s in range(3)] for p in range(4)]
    peers = [[[mixed([peer[a][d] for a in range(3)], p, s) for d in range(4)] for s in range(3)] for p in range(4)]
    barrier = pltpu.get_barrier_semaphore()
    for a in range(3):
        for d in range(1, 4):
            pl.semaphore_signal(barrier, inc=1, device_id=(core, peer[a][d]), device_id_type=MESH)
    pl.semaphore_wait(barrier, 9)
    sends = []

    def remote(src, dst, phase, p, d, stage):
        return pltpu.make_async_remote_copy(
            src_ref=src, dst_ref=dst, send_sem=send_sem.at[phase, p, d - 1], recv_sem=recv_sem.at[phase, p, d - 1],
            device_id=(core, peers[p][stage][d]), device_id_type=MESH)

    def go(*args):
        copy = remote(*args)
        copy.start()
        sends.append(copy)

    own = []
    for p in range(4):
        for d in (2, 1, 3):
            go(part_ref.at[lax.rem(mine[p][0] + d, 4), p], r1.at[p, d - 1], 0, p, d, 0)
    for p in range(4):
        copy = pltpu.make_async_copy(part_ref.at[mine[p][0], p], own_s.at[p], own_sem.at[p])
        copy.start()
        own.append(copy)
    lane = lax.broadcasted_iota(jnp.int32, (16, 128), 1)

    def top_tile(top):
        hi = top.astype(bf16).astype(f32)
        mid = (top - hi).astype(bf16).astype(f32)
        low = top - hi - mid
        return jnp.where(lane == 0, hi, jnp.where(lane == 1, mid, jnp.where(lane == 2, low, 0.0))).astype(bf16)

    def read_top(tile):
        return jnp.sum(tile.astype(f32), axis=1, keepdims=True)

    def merged(tops):
        top = functools.reduce(jnp.maximum, tops)
        return top, [jnp.exp(t - top) for t in tops]

    tops1 = []
    for p in range(4):
        own[p].wait()
        for d in (1, 2, 3):
            remote(own_s.at[p], r1.at[p, d - 1], 0, p, d, 0).wait_recv()
        sources = [own_s.at[p]] + [r1.at[p, d] for d in range(3)]
        top, gains = merged([read_top(s[16]) for s in sources])
        tops1.append(top)
        tile = top_tile(top)
        for j in range(4):
            for i in range(4):
                total = sum(g * s[4 * j + i].astype(f32) for g, s in zip(gains, sources))
                s1f[p, j, i] = total
                s2[p, j, i] = total.astype(bf16)
            s2[p, j, 4] = tile
        for d in (2, 1, 3):
            go(s2.at[p, lax.rem(mine[p][1] + d, 4)], r2.at[p, d - 1], 1, p, d, 1)
    tops2 = []
    for p in range(4):
        for d in (1, 2, 3):
            remote(s2.at[p, 0], r2.at[p, d - 1], 1, p, d, 1).wait_recv()
        top, gains = merged([tops1[p]] + [read_top(r2[p, d, 4]) for d in range(3)])
        tops2.append(top)
        tile = top_tile(top)
        for i in range(4):
            total = gains[0] * s1f[p, mine[p][1], i]
            for d in range(3):
                total += gains[d + 1] * r2[p, d, i].astype(f32)
            s2f[p, i] = total
            s3[p, i, 0] = total.astype(bf16)
            s3[p, i, 1] = tile
        for d in (2, 1, 3):
            go(s3.at[p, lax.rem(mine[p][2] + d, 4)], r3.at[p, d - 1], 2, p, d, 2)
    for p in range(4):
        for d in (1, 2, 3):
            remote(s3.at[p, 0], r3.at[p, d - 1], 2, p, d, 2).wait_recv()
        top, gains = merged([tops2[p]] + [read_top(r3[p, d, 1]) for d in range(3)])
        total = gains[0] * s2f[p, mine[p][2]]
        for d in range(3):
            total += gains[d + 1] * r3[p, d, 0].astype(f32)
        spot = out_ref.at[p, mine[p][0], mine[p][1], mine[p][2]]
        spot[...] = total.astype(bf16)
        for d in (2, 1, 3):
            go(spot, spot, 3, p, d, 2)
    for p in range(4):
        for d in (1, 2, 3):
            spot = out_ref.at[p, mine[p][0], mine[p][1], lax.rem(mine[p][2] + 4 - d, 4)]
            remote(spot, spot, 3, p, d, 2).wait_recv()
        spot = out_ref.at[p, mine[p][0], mine[p][1]]
        for d in (2, 1, 3):
            go(spot, spot, 4, p, d, 1)
    for p in range(4):
        for d in (1, 2, 3):
            spot = out_ref.at[p, mine[p][0], lax.rem(mine[p][1] + 4 - d, 4)]
            remote(spot, spot, 4, p, d, 1).wait_recv()
        spot = out_ref.at[p, mine[p][0]]
        for d in (2, 1, 3):
            go(spot, spot, 5, p, d, 0)
    for p in range(4):
        for d in (1, 2, 3):
            spot = out_ref.at[p, lax.rem(mine[p][0] + 4 - d, 4)]
            remote(spot, spot, 5, p, d, 0).wait_recv()
    for copy in sends:
        copy.wait_send()


def exchange_call(part):
    return pl.pallas_call(
        exchange_kernel,
        in_specs=[pl.BlockSpec(memory_space=pl.ANY)],
        out_specs=pl.BlockSpec(memory_space=pltpu.VMEM),
        out_shape=jax.ShapeDtypeStruct((4, 4, 4, 4, 16, 128), bf16),
        scratch_shapes=[
            pltpu.VMEM((4, 17, 16, 128), bf16),
            pltpu.VMEM((4, 3, 17, 16, 128), bf16),
            pltpu.VMEM((4, 4, 4, 16, 128), f32),
            pltpu.VMEM((4, 4, 5, 16, 128), bf16),
            pltpu.VMEM((4, 3, 5, 16, 128), bf16),
            pltpu.VMEM((4, 4, 16, 128), f32),
            pltpu.VMEM((4, 4, 2, 16, 128), bf16),
            pltpu.VMEM((4, 3, 2, 16, 128), bf16),
            pltpu.SemaphoreType.DMA((4,)),
            pltpu.SemaphoreType.DMA((6, 4, 3)),
            pltpu.SemaphoreType.DMA((6, 4, 3)),
        ],
        compiler_params=pltpu.CompilerParams(collective_id=1, has_side_effects=True, vmem_limit_bytes=32 * 2**20),
    )(part)


def norm_kernel(sum_ref, out_ref):
    tiles = [sum_ref[0, 0, n].astype(f32) for n in range(32)]
    square = sum(t * t for t in tiles)
    mean = jnp.sum(square, axis=1, keepdims=True) * (1.0 / 4096)
    scale = 1.0 / jnp.sqrt(mean + 1e-06)
    for n in range(32):
        out_ref[0, :, 128 * n:128 * n + 128] = tiles[n] * scale


def norm_call(summed):
    return pl.pallas_call(
        norm_kernel, grid=(2, 4),
        in_specs=[pl.BlockSpec((1, 1, 32, 16, 128), lambda w, p: (p, w, 0, 0, 0))],
        out_specs=pl.BlockSpec((1, 16, 4096), lambda w, p: (w, p, 0)),
        out_shape=jax.ShapeDtypeStruct((2, 64, 4096), f32),
    )(summed.reshape(4, 2, 32, 16, 128))


def on_device(tokens, lengths, feature_table, short_filter, long_filter, queries):
    first = (lax.axis_index("ctx") * 256).astype(jnp.int32).reshape(1)
    hot, tab = prep_call(tokens, feature_table, short_filter)
    mixer_field, part = main_call(first, lengths, hot, tab, long_filter, queries)
    return mixer_field, norm_call(exchange_call(part))


def solution(mesh):
    return jax.shard_map(
        on_device,
        mesh=mesh,
        in_specs=(P("batch", "ctx"), P("batch"), P(), P(), P(), P()),
        out_specs=(P("batch", "ctx", None), P("batch", None, None)),
        check_vma=False,
    )
```

time: 721 us -> 83.9 us (0.12)
  local copies, waits for them, and re-layouts: 275 us -> 7.15 us
  blocking collectives: 179 us -> 0 us
  waiting for transfers between devices: 128 us -> 0 us
  other arithmetic: 77.4 us -> 0 us
  Pallas kernels: 0 us -> 75.7 us
  matrix products: 35.6 us -> 0 us
  between operations: 14.2 us -> 0.7 us
  starting transfers between devices: 9.25 us -> 0 us
    gather x4 -> x0, local copies, waits for them, and re-layouts: 197 us -> none  [the longest x2 153 us: kernel_rows(): picked = jnp.take(long_filter, jnp.clip(offset, 0, tap_count - 1), axis=1)]
    pmax x1 -> x0, blocking collectives: 179 us -> none  [on_device(): row_top = lax.pmax(local_top, 'ctx')]
    psum x1 -> x0, waiting for transfers between devices: 120 us -> none  [on_device(): summed = lax.psum(weighted, 'ctx')]
    pallas_call x0 -> x4, Pallas kernels: none -> 75.7 us  [the longest x1 33.4 us: exchange_call(): pl.pallas_call(exchange_kernel, in_specs=[pl.BlockSpec(memory_space=pl.AN...]
    dot_general x4 -> x0, matrix products: 35.6 us -> none  [the longest x1 16.1 us: long_pass(): jnp.einsum('gim,wbmgc->wbigc', kernel[:, :, :tap_count], previous, prefer...]
    add x3 -> x0, other arithmetic: 32.2 us -> none  [the longest x1 32.2 us: short_pass(): short_filter[0] * source[:, 2:] + short_filter[1] * source[:, 1:count + 1]]
    reshape x3 -> x0, local copies, waits for them, and re-layouts: 25.3 us -> none  [the longest x1 11.5 us: long_pass(): return result.reshape(windows, row_count, model_width)]
    select_n x2 -> x0, other arithmetic: 21 us -> none  [the longest x1 14.3 us: kernel_rows(): return jnp.where(usable[None], picked, jnp.zeros_like(picked))]
  transfers between devices with their start and end apart: 3 -> 0, of which waited for: 2 -> 0; matrix products, arithmetic and copies ran while one was open for 27% -> 0% of each run, Pallas kernels for 0% -> 0%
where the time goes in v1:
time: 83.9 us; the launch traced here: 83.6 us
  Pallas kernels  75.7 us (90%)
  local copies, waits for them, and re-layouts  7.15 us (9%)
    pallas_call x1, Pallas kernels, exchange_call(): pl.pallas_call(exchange_kernel, in_specs=[pl.BlockSpec(memory_space=pl.AN...  33.4 us
    pallas_call x1, Pallas kernels, main_call(): pl.pallas_call(main_kernel, grid=(n,), in_specs=[smem, smem, pl.BlockSpec...  20.3 us
    pallas_call x1, Pallas kernels, prep_call(): pl.pallas_call(prep_kernel, in_specs=[vmem, pl.BlockSpec(memory_space=pl....  16.3 us
    unnamed x14, local copies, waits for them, and re-layouts  7.15 us
    pallas_call x1, Pallas kernels, norm_call(): pl.pallas_call(norm_kernel, grid=(2, 4), in_specs=[pl.BlockSpec((1, 1, 32...  5.8 us

profile of v1, /device:TPU:0, one launch (start us, length us, event | category | flops | bytes accessed | tf_op | source)
XLA Modules:
  0.0 83.6 jit_solution(3298575778224756644)
XLA Ops:
  0.6 0.0 copy-start
  0.6 4.6 %copy-done = bf16[512,12288]{1,0:T(8,128)(2,1)S(1)} copy-done((bf16[512,12288]{1,0:T(8,128)(2,1)S(1)}, bf16[512,12288]{1,0:T(8,128)(2,1)}, u32[]{:S(2)}) %copy-start) | copy-done | bytes 12582936
  5.2 0.0 copy-start.3
  5.2 0.9 %copy-done.3 = f32[3,12288]{1,0:T(4,128)S(1)} copy-done((f32[3,12288]{1,0:T(4,128)S(1)}, f32[3,12288]{1,0:T(4,128)}, u32[]{:S(2)}) %copy-start.3) | copy-done | bytes 147480
  6.1 0.0 copy-start.5
  6.1 0.7 copy-done.5
  6.8 0.0 copy-start.2
  6.8 0.0 copy-start.4
  6.8 0.0 copy-start.6
  6.8 16.3 %shard_map.77 = (bf16[80,768]{1,0:T(8,128)(2,1)S(1)}, bf16[12288,128]{1,0:T(8,128)(2,1)S(1)}) custom-call(s32[2,256]{1,0:T(2,128)S(1)} %copy-done.5, bf16[512,12288]{1,0:T(8,128)(2,1)S(1)} %copy-done, f32[3,12288]{1,0:T(4,128)S(1)} %copy-done.3), custom_call_target="tpu_custom_call" | custom-call | tf_op jit(solution)/shard_map/pallas_call | solution.py:75
  23.1 0.0 copy-done.2
  23.1 0.0 copy-done.4
  23.1 0.0 copy-done.6
  23.1 20.3 %shard_map.78 = (bf16[2,256,4096]{2,1,0:T(8,128)(2,1)}, bf16[4,4,17,16,128]{4,3,2,1,0:T(8,128)(2,1)S(1)}) custom-call(s32[1]{0:T(128)} %bitcast.first_ref, s32[2]{0:T(128)S(1)} %copy-done.6, bf16[80,768]{1,0:T(8,128)(2,1)S(1)} %get-tuple-element.6.oh_ref, bf16[12288,128]{1,0:T(8,128)(2,1)S(1)} %get-tuple-element.7.tq_ref.tk_ref.tv_ref, ...), custom_call_target="tpu_custom_call" | custom-call | tf_op jit(solution)/shard_map/pallas_call | solution.py:155
  43.4 33.4 %shard_map.79 = bf16[4,4,4,4,16,128]{5,4,3,2,1,0:T(8,128)(2,1)S(1)} custom-call(bf16[4,4,17,16,128]{4,3,2,1,0:T(8,128)(2,1)S(1)} %get-tuple-element.9.part_ref), custom_call_target="tpu_custom_call" | custom-call | tf_op jit(solution)/shard_map/pallas_call | solution.py:291
  76.8 0.0 copy-start.1
  76.8 1.0 %copy-done.1 = bf16[4,4,4,4,16,128]{5,4,3,2,1,0:T(8,128)(2,1)} copy-done((bf16[4,4,4,4,16,128]{5,4,3,2,1,0:T(8,128)(2,1)}, bf16[4,4,4,4,16,128]{5,4,3,2,1,0:T(8,128)(2,1)S(1)}, u32[]{:S(2)}) %copy-start.1) | copy-done | bytes 1048600
  77.8 5.8 %shard_map.80 = f32[2,64,4096]{2,1,0:T(8,128)} custom-call(bf16[4,2,32,16,128]{4,3,2,1,0:T(8,128)(2,1)} %bitcast.2), custom_call_target="tpu_custom_call" | custom-call | tf_op jit(solution)/shard_map/pallas_call | solution.py:323
Async XLA Ops:
  0.6 4.6 %copy-start = (bf16[512,12288]{1,0:T(8,128)(2,1)S(1)}, bf16[512,12288]{1,0:T(8,128)(2,1)}, u32[]{:S(2)}) copy-start(bf16[512,12288]{1,0:T(8,128)(2,1)} %table_ref.1) | copy-start | bytes 37748740
  5.2 0.9 %copy-start.3 = (f32[3,12288]{1,0:T(4,128)S(1)}, f32[3,12288]{1,0:T(4,128)}, u32[]{:S(2)}) copy-start(f32[3,12288]{1,0:T(4,128)} %sf_ref.1) | copy-start | bytes 442372
  6.1 0.7 copy-start.5
  6.8 16.3 %copy-start.2 = (bf16[64,4096]{1,0:T(8,128)(2,1)S(1)}, bf16[64,4096]{1,0:T(8,128)(2,1)}, u32[]{:S(2)}) copy-start(bf16[64,4096]{1,0:T(8,128)(2,1)} %qry_ref.1) | copy-start | bytes 1572868
  6.8 16.3 %copy-start.4 = (bf16[256,128]{1,0:T(8,128)(2,1)S(1)}, bf16[256,128]{1,0:T(8,128)(2,1)}, u32[]{:S(2)}) copy-start(bf16[256,128]{1,0:T(8,128)(2,1)} %h_ref.1) | copy-start | bytes 196612
  6.8 16.3 %copy-start.6 = (s32[2]{0:T(128)S(1)}, s32[2]{0:T(128)}, u32[]{:S(2)}) copy-start(s32[2]{0:T(128)} %len_ref.1) | copy-start | bytes 28
  76.8 1.0 %copy-start.1 = (bf16[4,4,4,4,16,128]{5,4,3,2,1,0:T(8,128)(2,1)}, bf16[4,4,4,4,16,128]{5,4,3,2,1,0:T(8,128)(2,1)S(1)}, u32[]{:S(2)}) copy-start(bf16[4,4,4,4,16,128]{5,4,3,2,1,0:T(8,128)(2,1)S(1)} %shard_map.79) | copy-start | bytes 3145732

commit v2 on v1

v2 whole, which is shorter than its diff:
```python
import functools

import jax
import jax.numpy as jnp
from jax import lax
from jax.experimental import pallas as pl
from jax.experimental.pallas import tpu as pltpu
from jax.sharding import PartitionSpec as P

bf16, f32 = jnp.bfloat16, jnp.float32
CODES = (65, 67, 71, 84, 97, 99, 103, 116)
STRIDES = (16, 4, 1)
MESH = pl.DeviceIdType.MESH
CB = 512
WIDE = 1024
GPC = CB // 16
T = 128
LOWEST = -1e38


def prep_kernel(tok_hbm, rows_s, sf_hbm, oh_ref, tab_ref, sf_s, tok_s, prev_s, sf_sem, tok_sem,
                send_sem, recv_sem):
    me = lax.axis_index("ctx")
    core = lax.axis_index("batch")
    nxt, prv = lax.rem(me + 1, 64), lax.rem(me + 63, 64)
    barrier = pltpu.get_barrier_semaphore()
    pl.semaphore_signal(barrier, inc=1, device_id=(core, prv), device_id_type=MESH)
    load_tok = pltpu.make_async_copy(tok_hbm, tok_s, tok_sem)
    load_tok.start()
    load_sf = pltpu.make_async_copy(sf_hbm, sf_s, sf_sem)
    load_sf.start()
    sel_row = lax.broadcasted_iota(jnp.int32, (32, 64), 0)
    sel_col = lax.broadcasted_iota(jnp.int32, (32, 64), 1)
    want = jnp.full((32, 64), -1, jnp.int32)
    for n in range(24):
        want = jnp.where(sel_row == n, CODES[n % 8] - 64, want)
    select = jnp.where(sel_col == want, 1.0, 0.0).astype(bf16)
    e_r = lax.broadcasted_iota(jnp.int32, (T, T), 0)
    e_c = lax.broadcasted_iota(jnp.int32, (T, T), 1)
    eye = jnp.where(e_r == e_c, 1.0, 0.0).astype(bf16)
    load_tok.wait()
    pl.semaphore_wait(barrier, 1)
    send = pltpu.make_async_remote_copy(
        src_ref=tok_s, dst_ref=prev_s, send_sem=send_sem, recv_sem=recv_sem,
        device_id=(core, nxt), device_id_type=MESH)
    send.start()
    load_sf.wait()

    @pl.loop(0, 12288 // WIDE)
    def _(step):
        base = pl.multiple_of(step * WIDE, WIDE)
        cols = pl.ds(base, WIDE)
        picked = jnp.dot(select, rows_s[:, cols], preferred_element_type=f32)[:24]
        gains = jnp.concatenate([jnp.broadcast_to(sf_s[n:n + 1, cols], (8, WIDE)) for n in range(3)], axis=0)
        prod = picked * gains
        hi = prod.astype(bf16).astype(f32)
        rest = prod - hi
        mid = rest.astype(bf16).astype(f32)
        low = rest - mid
        stacked = jnp.concatenate([hi, mid, low, jnp.zeros((56, WIDE), f32)], axis=0).astype(bf16)
        for u in range(WIDE // T):
            turned = lax.dot_general(eye, stacked[:, T * u:T * u + T], (((1,), (1,)), ((), ())),
                                     preferred_element_type=f32)
            tab_ref[pl.ds(base + T * u, T), :] = turned.astype(bf16)

    codes = jnp.zeros((8, 384), jnp.int32)
    code_row = lax.broadcasted_iota(jnp.int32, (8, 384), 0)
    for n in range(8):
        codes = jnp.where(code_row == n, CODES[n], codes)
    send.wait()
    prev = jnp.where(me == 0, -1, prev_s[...])
    for w in range(2):
        ext = jnp.concatenate([prev[w:w + 1], tok_s[w:w + 1]], axis=1)
        hot = [jnp.where(jnp.broadcast_to(ext[:, 128 - k:512 - k], (8, 384)) == codes, 1.0, 0.0) for k in range(3)]
        full = jnp.concatenate(hot * 3 + [jnp.zeros((8, 384), f32)], axis=0).astype(bf16)
        oh_ref[:, 128 * w:128 * w + 128] = full[:, :128]
        oh_ref[:, 256 + 256 * w:512 + 256 * w] = full[:, 128:]


def prep_call(tokens, table, short_filter):
    vmem = pl.BlockSpec(memory_space=pltpu.VMEM)
    hbm = pl.BlockSpec(memory_space=pltpu.HBM)
    return pl.pallas_call(
        prep_kernel,
        in_specs=[hbm, vmem, hbm],
        out_specs=[vmem, vmem],
        out_shape=[jax.ShapeDtypeStruct((80, 768), bf16), jax.ShapeDtypeStruct((12288, 128), bf16)],
        scratch_shapes=[pltpu.VMEM((3, 12288), f32), pltpu.VMEM((2, 256), jnp.int32),
                        pltpu.VMEM((2, 256), jnp.int32)] + [pltpu.SemaphoreType.DMA] * 4,
        compiler_params=pltpu.CompilerParams(collective_id=0, has_side_effects=True, vmem_limit_bytes=32 * 2**20),
    )(tokens, lax.slice(table, (64, 0), (128, 12288)), short_filter)


def main_kernel(oh_ref, tq_ref, tk_ref, tv_ref, h_ref, qry_ref, mix_ref, m_ref, s_ref, g_s):
    i = pl.program_id(0)
    oh = oh_ref[...]
    dot = functools.partial(jnp.dot, preferred_element_type=f32)
    k = dot(tk_ref[...][:, :80], oh)
    v = dot(tv_ref[...][:, :80], oh)
    g_s[...] = (k * v).astype(bf16)
    s_i = lax.broadcasted_iota(jnp.int32, (T, T), 0)
    t_i = lax.broadcasted_iota(jnp.int32, (T, T), 1)
    upper = t_i >= s_i
    h = h_ref[...].astype(f32)
    gate = dot(tq_ref[...][:, :80], oh[:, 256:])
    for j in range(GPC):
        circ = pltpu.roll(jnp.broadcast_to(h[j:j + 1], (T, T)), 0, 1, stride=1, stride_axis=0)
        toep = jnp.concatenate([jnp.where(upper, 0.0, circ), jnp.where(upper, circ, 0.0)], axis=0).astype(bf16)
        rows = pl.ds(16 * j, 16)
        q = gate[16 * j:16 * j + 16]
        blk = [g_s[rows, pl.ds(T * b, T)] for b in range(6)]
        lhs = jnp.concatenate([
            jnp.concatenate([blk[0], blk[2]], axis=1),
            jnp.concatenate([blk[2], blk[3]], axis=1),
            jnp.concatenate([blk[1], blk[4]], axis=1),
            jnp.concatenate([blk[4], blk[5]], axis=1)], axis=0)
        conv = dot(lhs, toep)
        conv = jnp.concatenate([conv[16 * b:16 * b + 16] for b in range(4)], axis=1)
        m_ref[rows, :] = (q * conv).astype(bf16)
    m = m_ref[...]
    sc = dot(qry_ref[...], m)

    @pl.when(i == 0)
    def _():
        s_ref[...] = sc

    @pl.when(i > 0)
    def _():
        s_ref[...] += sc
    for w in range(2):
        mix_ref[w] = m[:, 256 * w:256 * w + 256].T


def main_call(oh, tab, h, qry):
    n = 4096 // CB
    return pl.pallas_call(
        main_kernel, grid=(n,),
        in_specs=[
            pl.BlockSpec((80, 768), lambda i: (0, 0)),
            pl.BlockSpec((CB, 128), lambda i: (i, 0)),
            pl.BlockSpec((CB, 128), lambda i: (i + n, 0)),
            pl.BlockSpec((CB, 128), lambda i: (i + 2 * n, 0)),
            pl.BlockSpec((GPC, 128), lambda i: (i, 0)),
            pl.BlockSpec((64, CB), lambda i: (0, i))],
        out_specs=[pl.BlockSpec((2, 256, CB), lambda i: (0, 0, i)),
                   pl.BlockSpec((CB, 512), lambda i: (i, 0)),
                   pl.BlockSpec((64, 512), lambda i: (0, 0))],
        out_shape=[jax.ShapeDtypeStruct((2, 256, 4096), bf16), jax.ShapeDtypeStruct((4096, 512), bf16),
                   jax.ShapeDtypeStruct((64, 512), f32)],
        scratch_shapes=[pltpu.VMEM((CB, 768), bf16)],
        compiler_params=pltpu.CompilerParams(vmem_limit_bytes=32 * 2**20, dimension_semantics=("arbitrary",)),
    )(oh, tab, tab, tab, h, qry)


def exchange_kernel(len_ref, s_ref, m_ref, out_ref, part_s, r1, s1f, s2, r2, r3, send_sem, recv_sem):
    me = lax.axis_index("ctx")
    core = lax.axis_index("batch")
    coord = [lax.rem(me // st, 4) for st in STRIDES]
    peer = [[me + (lax.rem(coord[a] + d, 4) - coord[a]) * STRIDES[a] for d in range(4)] for a in range(3)]

    def mixed(values, p, stage):
        first, second = values[(p + stage) % 3], values[(p + stage + 1) % 3]
        return first + core * (second - first)

    mine = [[mixed(coord, p, s) for s in range(3)] for p in range(4)]
    peers = [[[mixed([peer[a][d] for a in range(3)], p, s) for d in range(4)] for s in range(3)] for p in range(4)]
    barrier = pltpu.get_barrier_semaphore()
    for a in range(3):
        for d in range(1, 4):
            pl.semaphore_signal(barrier, inc=1, device_id=(core, peer[a][d]), device_id_type=MESH)
    lane = lax.broadcasted_iota(jnp.int32, (16, 128), 1)

    def top_tile(top):
        hi = top.astype(bf16).astype(f32)
        mid = (top - hi).astype(bf16).astype(f32)
        low = top - hi - mid
        return jnp.where(lane == 0, hi, jnp.where(lane == 1, mid, jnp.where(lane == 2, low, 0.0))).astype(bf16)

    position = lax.broadcasted_iota(jnp.int32, (64, 256), 1) + me * 256
    for w in range(2):
        half = slice(256 * w, 256 * w + 256)
        scores = s_ref[:, half] * (4096 ** -0.5)
        valid = position < len_ref[w]
        top = jnp.max(jnp.where(valid, scores, LOWEST), axis=1, keepdims=True)
        shifted = jnp.where(valid, scores - top, 0.0)
        weights = jnp.where(valid, jnp.exp(shifted), 0.0).astype(bf16)
        for c in range(16):
            summed = lax.dot_general(weights, m_ref[256 * c:256 * c + 256, half], (((1,), (1,)), ((), ())),
                                     preferred_element_type=f32).astype(bf16)
            for p in range(4):
                for u in range(2):
                    part_s[2 * w + c // 8, p, 2 * (c % 8) + u] = summed[16 * p:16 * p + 16, T * u:T * u + T]
        for p in range(4):
            tile = top_tile(top[16 * p:16 * p + 16])
            for n in range(2):
                part_s[2 * w + n, p, 16] = tile
    pl.semaphore_wait(barrier, 9)
    sends = []

    def remote(src, dst, phase, p, d, stage):
        return pltpu.make_async_remote_copy(
            src_ref=src, dst_ref=dst, send_sem=send_sem.at[phase, p, d - 1], recv_sem=recv_sem.at[phase, p, d - 1],
            device_id=(core, peers[p][stage][d]), device_id_type=MESH)

    def go(*args):
        copy = remote(*args)
        copy.start()
        sends.append(copy)

    for p in range(4):
        for d in (2, 1, 3):
            go(part_s.at[lax.rem(mine[p][0] + d, 4), p], r1.at[p, d - 1], 0, p, d, 0)

    def read_top(tile):
        return jnp.sum(tile.astype(f32), axis=1, keepdims=True)

    def merged(tops):
        top = functools.reduce(jnp.maximum, tops)
        return top, [jnp.exp(t - top) for t in tops]

    tops1 = []
    for p in range(4):
        own = part_s.at[mine[p][0], p]
        for d in (1, 2, 3):
            remote(own, r1.at[p, d - 1], 0, p, d, 0).wait_recv()
        sources = [own] + [r1.at[p, d] for d in range(3)]
        top, gains = merged([read_top(s[16]) for s in sources])
        tops1.append(top)
        tile = top_tile(top)
        for j in range(4):
            for i in range(4):
                total = sum(g * s[4 * j + i].astype(f32) for g, s in zip(gains, sources))
                s1f[p, j, i] = total
                s2[p, j, i] = total.astype(bf16)
            s2[p, j, 4] = tile
        for d in (2, 1, 3):
            go(s2.at[p, lax.rem(mine[p][1] + d, 4)], r2.at[p, d - 1], 1, p, d, 1)
    for p in range(4):
        for d in (1, 2, 3):
            remote(s2.at[p, 0], r2.at[p, d - 1], 1, p, d, 1).wait_recv()
        top, gains = merged([tops1[p]] + [read_top(r2[p, d, 4]) for d in range(3)])
        here = r3.at[p, mine[p][2]]
        here[4] = top_tile(top)
        for i in range(4):
            total = gains[0] * s1f[p, mine[p][1], i]
            for d in range(3):
                total += gains[d + 1] * r2[p, d, i].astype(f32)
            here[i] = total.astype(bf16)
        for d in (2, 1, 3):
            go(here, here, 2, p, d, 2)
    for p in range(4):
        for d in (1, 2, 3):
            there = r3.at[p, lax.rem(mine[p][2] + 4 - d, 4)]
            remote(there, there, 2, p, d, 2).wait_recv()
        top, gains = merged([read_top(r3[p, k, 4]) for k in range(4)])
        spot = out_ref.at[p, mine[p][0], mine[p][1]]
        for i in range(4):
            total = gains[0] * r3[p, 0, i].astype(f32)
            for k in range(1, 4):
                total += gains[k] * r3[p, k, i].astype(f32)
            spot[i] = total.astype(bf16)
        for d in (2, 1, 3):
            go(spot, spot, 3, p, d, 1)
    for p in range(4):
        for d in (1, 2, 3):
            spot = out_ref.at[p, mine[p][0], lax.rem(mine[p][1] + 4 - d, 4)]
            remote(spot, spot, 3, p, d, 1).wait_recv()
        spot = out_ref.at[p, mine[p][0]]
        for d in (2, 1, 3):
            go(spot, spot, 4, p, d, 0)
    for p in range(4):
        for d in (1, 2, 3):
            spot = out_ref.at[p, lax.rem(mine[p][0] + 4 - d, 4)]
            remote(spot, spot, 4, p, d, 0).wait_recv()
    for copy in sends:
        copy.wait_send()


def exchange_call(lengths, scores, field):
    vmem = pl.BlockSpec(memory_space=pltpu.VMEM)
    return pl.pallas_call(
        exchange_kernel,
        in_specs=[pl.BlockSpec(memory_space=pltpu.SMEM), vmem, vmem],
        out_specs=vmem,
        out_shape=jax.ShapeDtypeStruct((4, 4, 4, 4, 16, 128), bf16),
        scratch_shapes=[
            pltpu.VMEM((4, 4, 17, 16, 128), bf16),
            pltpu.VMEM((4, 3, 17, 16, 128), bf16),
            pltpu.VMEM((4, 4, 4, 16, 128), f32),
            pltpu.VMEM((4, 4, 5, 16, 128), bf16),
            pltpu.VMEM((4, 3, 5, 16, 128), bf16),
            pltpu.VMEM((4, 4, 5, 16, 128), bf16),
            pltpu.SemaphoreType.DMA((5, 4, 3)),
            pltpu.SemaphoreType.DMA((5, 4, 3)),
        ],
        compiler_params=pltpu.CompilerParams(collective_id=1, has_side_effects=True, vmem_limit_bytes=32 * 2**20),
    )(lengths, scores, field)


def norm_kernel(sum_ref, out_ref):
    for p in range(4):
        tiles = [sum_ref[p, 0, n].astype(f32) for n in range(32)]
        square = sum(t * t for t in tiles)
        mean = jnp.sum(square, axis=1, keepdims=True) * (1.0 / 4096)
        scale = 1.0 / jnp.sqrt(mean + 1e-06)
        for n in range(32):
            out_ref[0, 16 * p:16 * p + 16, 128 * n:128 * n + 128] = tiles[n] * scale


def norm_call(summed):
    return pl.pallas_call(
        norm_kernel, grid=(2,),
        in_specs=[pl.BlockSpec((4, 1, 32, 16, 128), lambda w: (0, w, 0, 0, 0))],
        out_specs=pl.BlockSpec((1, 64, 4096), lambda w: (w, 0, 0)),
        out_shape=jax.ShapeDtypeStruct((2, 64, 4096), f32),
        compiler_params=pltpu.CompilerParams(vmem_limit_bytes=16 * 2**20),
    )(summed.reshape(4, 2, 32, 16, 128))


def on_device(tokens, lengths, feature_table, short_filter, long_filter, queries):
    hot, tab = prep_call(tokens, feature_table, short_filter)
    mixer_field, field, scores = main_call(hot, tab, long_filter, queries)
    return mixer_field, norm_call(exchange_call(lengths, scores, field))


def solution(mesh):
    return jax.shard_map(
        on_device,
        mesh=mesh,
        in_specs=(P("batch", "ctx"), P("batch"), P(), P(), P(), P()),
        out_specs=(P("batch", "ctx", None), P("batch", None, None)),
        check_vma=False,
    )
```

time: 83.9 us -> 54.4 us (0.65)
  Pallas kernels: 75.7 us -> 50.3 us
  local copies, waits for them, and re-layouts: 7.15 us -> 3.19 us
    pallas_call x4, Pallas kernels: 75.7 us -> 50.3 us  [the longest x1 26.5 us: exchange_call(): pl.pallas_call(exchange_kernel, in_specs=[pl.BlockSpec(memory_space=pltpu...]
    unnamed x14 -> x10, local copies, waits for them, and re-layouts: 7.15 us -> 1.62 us
    slice x0 -> x1, local copies, waits for them, and re-layouts: none -> 1.57 us  [prep_call(): lax.slice(table, (64, 0), (128, 12288))]
where the time goes in v2:
time: 54.4 us; the launch traced here: 54.2 us
  Pallas kernels  50.3 us (92%)
  local copies, waits for them, and re-layouts  3.19 us (6%)
  between operations  0.7 us (1%)
    pallas_call x1, Pallas kernels, exchange_call(): pl.pallas_call(exchange_kernel, in_specs=[pl.BlockSpec(memory_space=pltpu...  26.5 us
    pallas_call x1, Pallas kernels, main_call(): pl.pallas_call(main_kernel, grid=(n,), in_specs=[pl.BlockSpec((80, 768),...  11.5 us
    pallas_call x1, Pallas kernels, prep_call(): pl.pallas_call(prep_kernel, in_specs=[hbm, vmem, hbm], out_specs=[vmem, v...  10.7 us
    unnamed x10, local copies, waits for them, and re-layouts  1.62 us
    pallas_call x1, Pallas kernels, norm_call(): pl.pallas_call(norm_kernel, grid=(2,), in_specs=[pl.BlockSpec((4, 1, 32,...  1.61 us
    slice x1, local copies, waits for them, and re-layouts, prep_call(): lax.slice(table, (64, 0), (128, 12288))  1.57 us

profile of v2, /device:TPU:0, one launch (start us, length us, event | category | flops | bytes accessed | tf_op | source)
XLA Modules:
  0.0 54.2 jit_solution(5522977701617018549)
XLA Ops:
  0.6 0.0 copy-start
  0.6 0.0 copy-start.2
  0.7 1.6 %slice.3.rows_s = bf16[64,12288]{1,0:T(8,128)(2,1)S(1)} slice(bf16[512,12288]{1,0:T(8,128)(2,1)} %param.8), slice={[64:128], [0:12288]} | slice | bytes 3145728 | tf_op jit(solution)/shard_map/slice | solution.py:91
  2.2 0.0 copy-start.1
  2.2 0.9 %copy-done.1 = f32[3,12288]{1,0:T(4,128)S(1)} copy-done((f32[3,12288]{1,0:T(4,128)S(1)}, f32[3,12288]{1,0:T(4,128)}, u32[]{:S(2)}) %copy-start.1) | copy-done | bytes 147480
  3.2 0.0 copy-start.3
  3.2 0.7 %copy-done.3 = s32[2,256]{1,0:T(2,128)S(1)} copy-done((s32[2,256]{1,0:T(2,128)S(1)}, s32[2,256]{1,0:T(2,128)}, u32[]{:S(2)}) %copy-start.3) | copy-done | bytes 2072
  3.8 10.7 %shard_map.77 = (bf16[80,768]{1,0:T(8,128)(2,1)S(1)}, bf16[12288,128]{1,0:T(8,128)(2,1)S(1)}) custom-call(s32[2,256]{1,0:T(2,128)S(1)} %copy-done.3, bf16[64,12288]{1,0:T(8,128)(2,1)S(1)} %slice.3.rows_s, f32[3,12288]{1,0:T(4,128)S(1)} %copy-done.1), custom_call_target="tpu_custom_call" | custom-call | tf_op jit(solution)/shard_map/pallas_call | solution.py:83
  14.5 0.0 copy-done
  14.6 0.0 copy-done.2
  14.6 0.0 copy-start.4
  14.6 11.5 %shard_map.78 = (bf16[2,256,4096]{2,1,0:T(8,128)(2,1)}, bf16[4096,512]{1,0:T(8,128)(2,1)S(1)}, f32[64,512]{1,0:T(8,128)S(1)}) custom-call(bf16[80,768]{1,0:T(8,128)(2,1)S(1)} %get-tuple-element.7.oh_ref, bf16[12288,128]{1,0:T(8,128)(2,1)S(1)} %get-tuple-element.8.tq_ref.tk_ref.tv_ref, bf16[12288,128]{1,0:T(8,128)(2,1)S(1)} %get-tuple-element.8.tq_ref.tk_ref.tv_ref, ...), custom_call_target="tpu_custom_call" | custom-call | tf_op jit(solution)/shard_map/pallas_call | solution.py:136
  26.0 0.0 copy-done.4
  26.0 26.5 %shard_map.79 = bf16[4,4,4,4,16,128]{5,4,3,2,1,0:T(8,128)(2,1)S(1)} custom-call(s32[2]{0:T(128)S(1)} %copy-done.4, f32[64,512]{1,0:T(8,128)S(1)} %get-tuple-element.10.s_ref, bf16[4096,512]{1,0:T(8,128)(2,1)S(1)} %get-tuple-element.11.m_ref), custom_call_target="tpu_custom_call" | custom-call | tf_op jit(solution)/shard_map/pallas_call | solution.py:281
  52.6 1.6 %shard_map.80 = f32[2,64,4096]{2,1,0:T(8,128)} custom-call(bf16[4,2,32,16,128]{4,3,2,1,0:T(8,128)(2,1)S(1)} %bitcast.1), custom_call_target="tpu_custom_call" | custom-call | tf_op jit(solution)/shard_map/pallas_call | solution.py:311
Async XLA Ops:
  0.6 13.9 %copy-start = (bf16[64,4096]{1,0:T(8,128)(2,1)S(1)}, bf16[64,4096]{1,0:T(8,128)(2,1)}, u32[]{:S(2)}) copy-start(bf16[64,4096]{1,0:T(8,128)(2,1)} %qry_ref.1) | copy-start | bytes 1572868
  0.6 13.9 %copy-start.2 = (bf16[256,128]{1,0:T(8,128)(2,1)S(1)}, bf16[256,128]{1,0:T(8,128)(2,1)}, u32[]{:S(2)}) copy-start(bf16[256,128]{1,0:T(8,128)(2,1)} %h_ref.1) | copy-start | bytes 196612
  2.2 0.9 %copy-start.1 = (f32[3,12288]{1,0:T(4,128)S(1)}, f32[3,12288]{1,0:T(4,128)}, u32[]{:S(2)}) copy-start(f32[3,12288]{1,0:T(4,128)} %sf_hbm.1) | copy-start | bytes 442372
  3.2 0.7 %copy-start.3 = (s32[2,256]{1,0:T(2,128)S(1)}, s32[2,256]{1,0:T(2,128)}, u32[]{:S(2)}) copy-start(s32[2,256]{1,0:T(2,128)} %tok_hbm.1) | copy-start | bytes 6148
  14.6 11.5 %copy-start.4 = (s32[2]{0:T(128)S(1)}, s32[2]{0:T(128)}, u32[]{:S(2)}) copy-start(s32[2]{0:T(128)} %len_ref.1) | copy-start | bytes 28

commit v3 on v2

v3 whole, which is shorter than its diff:
```python
import functools

import jax
import jax.numpy as jnp
from jax import lax
from jax.experimental import pallas as pl
from jax.experimental.pallas import tpu as pltpu
from jax.sharding import PartitionSpec as P

bf16, f32 = jnp.bfloat16, jnp.float32
CODES = (65, 67, 71, 84, 97, 99, 103, 116)
STRIDES = (16, 4, 1)
MESH = pl.DeviceIdType.MESH
CB = 1024
STEPS = 4096 // CB
UNIT = 256
WIDE = 1024
T = 128
LOWEST = -1e38
VMEM_LIMIT = 60 * 2**20


def build_tables(rows_s, sf_s, tab_s):
    sel_row = lax.broadcasted_iota(jnp.int32, (32, 64), 0)
    sel_col = lax.broadcasted_iota(jnp.int32, (32, 64), 1)
    want = jnp.full((32, 64), -1, jnp.int32)
    for n in range(24):
        want = jnp.where(sel_row == n, CODES[n % 8] - 64, want)
    select = jnp.where(sel_col == want, 1.0, 0.0).astype(bf16)
    e_r = lax.broadcasted_iota(jnp.int32, (T, T), 0)
    e_c = lax.broadcasted_iota(jnp.int32, (T, T), 1)
    eye = jnp.where(e_r == e_c, 1.0, 0.0).astype(bf16)

    @pl.loop(0, 12288 // WIDE)
    def _(step):
        base = pl.multiple_of(step * WIDE, WIDE)
        cols = pl.ds(base, WIDE)
        picked = jnp.dot(select, rows_s[:, cols], preferred_element_type=f32)[:24]
        gains = jnp.concatenate([jnp.broadcast_to(sf_s[n:n + 1, cols], (8, WIDE)) for n in range(3)], axis=0)
        prod = picked * gains
        hi = prod.astype(bf16).astype(f32)
        rest = prod - hi
        mid = rest.astype(bf16).astype(f32)
        low = rest - mid
        stacked = jnp.concatenate([hi, mid, low, jnp.zeros((56, WIDE), f32)], axis=0).astype(bf16)
        for u in range(WIDE // T):
            turned = lax.dot_general(eye, stacked[:, T * u:T * u + T], (((1,), (1,)), ((), ())),
                                     preferred_element_type=f32)
            tab_s[pl.ds(base + T * u, T), :] = turned.astype(bf16)


def build_hot(prev, tok_s, oh_s):
    codes = jnp.zeros((8, 384), jnp.int32)
    code_row = lax.broadcasted_iota(jnp.int32, (8, 384), 0)
    for n in range(8):
        codes = jnp.where(code_row == n, CODES[n], codes)
    for w in range(2):
        ext = jnp.concatenate([prev[w:w + 1], tok_s[w:w + 1]], axis=1)
        hot = [jnp.where(jnp.broadcast_to(ext[:, 128 - k:512 - k], (8, 384)) == codes, 1.0, 0.0) for k in range(3)]
        full = jnp.concatenate(hot * 3 + [jnp.zeros((8, 384), f32)], axis=0).astype(bf16)
        oh_s[:, 128 * w:128 * w + 128] = full[:, :128]
        oh_s[:, 256 + 256 * w:512 + 256 * w] = full[:, 128:]


def mix_block(step, tab_s, oh_s, h_s, qry_s, g_s, q_s, m_s, s_s, mix_s):
    dot = functools.partial(jnp.dot, preferred_element_type=f32)
    s_i = lax.broadcasted_iota(jnp.int32, (T, T), 0)
    t_i = lax.broadcasted_iota(jnp.int32, (T, T), 1)
    upper = t_i >= s_i
    base = pl.multiple_of(step * CB, CB)
    h = h_s[pl.ds(pl.multiple_of(step * (CB // 16), CB // 16), CB // 16), :].astype(f32)
    for u in range(CB // UNIT):
        rows = pl.ds(UNIT * u, UNIT)
        q, k, v = (dot(tab_s[pl.ds(4096 * n + base + UNIT * u, UNIT), :][:, :80], oh_s[:, 256:] if n == 0 else oh_s[...])
                   for n in range(3))
        g_s[rows, :] = (k * v).astype(bf16)
        q_s[rows, :] = q
    for j in range(CB // 16):
        circ = pltpu.roll(jnp.broadcast_to(h[j:j + 1], (T, T)), 0, 1, stride=1, stride_axis=0)
        toep = jnp.concatenate([jnp.where(upper, 0.0, circ), jnp.where(upper, circ, 0.0)], axis=0).astype(bf16)
        rows = pl.ds(16 * j, 16)
        blk = [g_s[rows, pl.ds(T * b, T)] for b in range(6)]
        lhs = jnp.concatenate([jnp.concatenate([blk[a], blk[b]], axis=1)
                               for a, b in ((0, 2), (2, 3), (1, 4), (4, 5))], axis=0)
        conv = dot(lhs, toep)
        conv = jnp.concatenate([conv[16 * b:16 * b + 16] for b in range(4)], axis=1)
        m_s[pl.ds(base + 16 * j, 16), :] = (q_s[rows, :] * conv).astype(bf16)
    for u in range(CB // UNIT):
        rows = pl.ds(base + UNIT * u, UNIT)
        m = m_s[rows, :]
        for w in range(2):
            mix_s[step, w, :, UNIT * u:UNIT * u + UNIT] = m[:, 256 * w:256 * w + 256].T
    s_s[...] += dot(qry_s[step], m_s[pl.ds(base, CB), :])


def layer_kernel(len_ref, tok_hbm, table_hbm, sf_hbm, h_hbm, qry_hbm, mix_out, sum_out,
                 tok_s, prev_s, rows_s, sf_s, h_s, qry_s, tab_s, oh_s, g_s, q_s, m_ref, s_ref, mix_s,
                 part_s, r1, s1f, s2, r2, r3, out_ref, load_sem, qry_sem, mix_sem, own_sem, tok_sem, send_sem, recv_sem):
    me = lax.axis_index("ctx")
    core = lax.axis_index("batch")
    coord = [lax.rem(me // st, 4) for st in STRIDES]
    peer = [[me + (lax.rem(coord[a] + d, 4) - coord[a]) * STRIDES[a] for d in range(4)] for a in range(3)]

    def mixed(values, p, stage):
        first, second = values[(p + stage) % 3], values[(p + stage + 1) % 3]
        return first + core * (second - first)

    mine = [[mixed(coord, p, s) for s in range(3)] for p in range(4)]
    peers = [[[mixed([peer[a][d] for a in range(3)], p, s) for d in range(4)] for s in range(3)] for p in range(4)]
    barrier = pltpu.get_barrier_semaphore()
    for a in range(3):
        for d in range(1, 4):
            pl.semaphore_signal(barrier, inc=1, device_id=(core, peer[a][d]), device_id_type=MESH)
    nxt, prv = lax.rem(me + 1, 64), lax.rem(me + 63, 64)
    pl.semaphore_signal(barrier, inc=1, device_id=(core, prv), device_id_type=MESH)
    loads = [pltpu.make_async_copy(src, dst, load_sem.at[n]) for n, (src, dst) in enumerate((
        (tok_hbm, tok_s), (sf_hbm, sf_s), (table_hbm.at[pl.ds(64, 64)], rows_s), (h_hbm, h_s)))]
    for n in range(STEPS):
        loads.append(pltpu.make_async_copy(qry_hbm.at[:, pl.ds(CB * n, CB)], qry_s.at[n], qry_sem.at[n]))
    for load in loads:
        load.start()
    s_ref[...] = jnp.zeros_like(s_ref)
    loads[0].wait()
    pl.semaphore_wait(barrier, 10)
    give = pltpu.make_async_remote_copy(
        src_ref=tok_s, dst_ref=prev_s, send_sem=tok_sem.at[0], recv_sem=tok_sem.at[1],
        device_id=(core, nxt), device_id_type=MESH)
    give.start()
    for load in loads[1:]:
        load.wait()
    build_tables(rows_s, sf_s, tab_s)
    give.wait()
    build_hot(jnp.where(me == 0, -1, prev_s[...]), tok_s, oh_s)

    @pl.loop(0, STEPS)
    def _(step):
        mix_block(step, tab_s, oh_s, h_s, qry_s, g_s, q_s, m_ref, s_ref, mix_s)

    writes = []
    for n in range(STEPS):
        write = pltpu.make_async_copy(mix_s.at[n], mix_out.at[:, :, pl.ds(CB * n, CB)], mix_sem.at[n])
        write.start()
        writes.append(write)
    lane = lax.broadcasted_iota(jnp.int32, (16, 128), 1)

    def top_tile(top):
        hi = top.astype(bf16).astype(f32)
        mid = (top - hi).astype(bf16).astype(f32)
        low = top - hi - mid
        return jnp.where(lane == 0, hi, jnp.where(lane == 1, mid, jnp.where(lane == 2, low, 0.0))).astype(bf16)

    position = lax.broadcasted_iota(jnp.int32, (64, 256), 1) + me * 256
    for w in range(2):
        half = slice(256 * w, 256 * w + 256)
        scores = s_ref[:, half] * (4096 ** -0.5)
        valid = position < len_ref[w]
        top = jnp.max(jnp.where(valid, scores, LOWEST), axis=1, keepdims=True)
        shifted = jnp.where(valid, scores - top, 0.0)
        weights = jnp.where(valid, jnp.exp(shifted), 0.0).astype(bf16)
        for c in range(16):
            summed = lax.dot_general(weights, m_ref[256 * c:256 * c + 256, half], (((1,), (1,)), ((), ())),
                                     preferred_element_type=f32).astype(bf16)
            for p in range(4):
                for u in range(2):
                    part_s[2 * w + c // 8, p, 2 * (c % 8) + u] = summed[16 * p:16 * p + 16, T * u:T * u + T]
        for p in range(4):
            tile = top_tile(top[16 * p:16 * p + 16])
            for n in range(2):
                part_s[2 * w + n, p, 16] = tile
    sends = []

    def remote(src, dst, phase, p, d, stage):
        return pltpu.make_async_remote_copy(
            src_ref=src, dst_ref=dst, send_sem=send_sem.at[phase, p, d - 1], recv_sem=recv_sem.at[phase, p, d - 1],
            device_id=(core, peers[p][stage][d]), device_id_type=MESH)

    def go(*args):
        copy = remote(*args)
        copy.start()
        sends.append(copy)

    for p in range(4):
        for d in (2, 1, 3):
            go(part_s.at[lax.rem(mine[p][0] + d, 4), p], r1.at[p, d - 1], 0, p, d, 0)

    def read_top(tile):
        return jnp.sum(tile.astype(f32), axis=1, keepdims=True)

    def merged(tops):
        top = functools.reduce(jnp.maximum, tops)
        return top, [jnp.exp(t - top) for t in tops]

    tops1 = []
    for p in range(4):
        own = part_s.at[mine[p][0], p]
        for d in (1, 2, 3):
            remote(own, r1.at[p, d - 1], 0, p, d, 0).wait_recv()
        sources = [own] + [r1.at[p, d] for d in range(3)]
        top, gains = merged([read_top(s[16]) for s in sources])
        tops1.append(top)
        tile = top_tile(top)
        for j in range(4):
            for i in range(4):
                total = sum(g * s[4 * j + i].astype(f32) for g, s in zip(gains, sources))
                s1f[p, j, i] = total
                s2[p, j, i] = total.astype(bf16)
            s2[p, j, 4] = tile
        for d in (2, 1, 3):
            go(s2.at[p, lax.rem(mine[p][1] + d, 4)], r2.at[p, d - 1], 1, p, d, 1)
    for p in range(4):
        for d in (1, 2, 3):
            remote(s2.at[p, 0], r2.at[p, d - 1], 1, p, d, 1).wait_recv()
        top, gains = merged([tops1[p]] + [read_top(r2[p, d, 4]) for d in range(3)])
        here = r3.at[p, mine[p][2]]
        here[4] = top_tile(top)
        for i in range(4):
            total = gains[0] * s1f[p, mine[p][1], i]
            for d in range(3):
                total += gains[d + 1] * r2[p, d, i].astype(f32)
            here[i] = total.astype(bf16)
        for d in (2, 1, 3):
            go(here, here, 2, p, d, 2)
    for p in range(4):
        for d in (1, 2, 3):
            there = r3.at[p, lax.rem(mine[p][2] + 4 - d, 4)]
            remote(there, there, 2, p, d, 2).wait_recv()
        top, gains = merged([read_top(r3[p, k, 4]) for k in range(4)])
        spot = out_ref.at[p, mine[p][0], mine[p][1]]
        for i in range(4):
            total = gains[0] * r3[p, 0, i].astype(f32)
            for k in range(1, 4):
                total += gains[k] * r3[p, k, i].astype(f32)
            spot[i] = total.astype(bf16)
        for d in (2, 1, 3):
            go(spot, spot, 3, p, d, 1)
    for p in range(4):
        for d in (1, 2, 3):
            spot = out_ref.at[p, mine[p][0], lax.rem(mine[p][1] + 4 - d, 4)]
            remote(spot, spot, 3, p, d, 1).wait_recv()
        spot = out_ref.at[p, mine[p][0]]
        for d in (2, 1, 3):
            go(spot, sum_out.at[p, mine[p][0]], 4, p, d, 0)
        keep = pltpu.make_async_copy(spot, sum_out.at[p, mine[p][0]], own_sem.at[p])
        keep.start()
        writes.append(keep)
    for p in range(4):
        for d in (1, 2, 3):
            spot = sum_out.at[p, lax.rem(mine[p][0] + 4 - d, 4)]
            remote(spot, spot, 4, p, d, 0).wait_recv()
    for copy in sends:
        copy.wait_send()
    for write in writes:
        write.wait()


def layer_call(lengths, tokens, table, short_filter, long_filter, queries):
    hbm = pl.BlockSpec(memory_space=pltpu.HBM)
    return pl.pallas_call(
        layer_kernel,
        in_specs=[pl.BlockSpec(memory_space=pltpu.SMEM)] + [hbm] * 5,
        out_specs=[hbm, hbm],
        out_shape=[jax.ShapeDtypeStruct((2, 256, 4096), bf16), jax.ShapeDtypeStruct((4, 4, 4, 4, 16, 128), bf16)],
        scratch_shapes=[
            pltpu.VMEM((2, 256), jnp.int32),
            pltpu.VMEM((2, 256), jnp.int32),
            pltpu.VMEM((64, 12288), bf16),
            pltpu.VMEM((3, 12288), f32),
            pltpu.VMEM((256, 128), bf16),
            pltpu.VMEM((STEPS, 64, CB), bf16),
            pltpu.VMEM((12288, 128), bf16),
            pltpu.VMEM((80, 768), bf16),
            pltpu.VMEM((CB, 768), bf16),
            pltpu.VMEM((CB, 512), f32),
            pltpu.VMEM((4096, 512), bf16),
            pltpu.VMEM((64, 512), f32),
            pltpu.VMEM((STEPS, 2, 256, CB), bf16),
            pltpu.VMEM((4, 4, 17, 16, 128), bf16),
            pltpu.VMEM((4, 3, 17, 16, 128), bf16),
            pltpu.VMEM((4, 4, 4, 16, 128), f32),
            pltpu.VMEM((4, 4, 5, 16, 128), bf16),
            pltpu.VMEM((4, 3, 5, 16, 128), bf16),
            pltpu.VMEM((4, 4, 5, 16, 128), bf16),
            pltpu.VMEM((4, 4, 4, 4, 16, 128), bf16),
            pltpu.SemaphoreType.DMA((4,)),
            pltpu.SemaphoreType.DMA((STEPS,)),
            pltpu.SemaphoreType.DMA((STEPS,)),
            pltpu.SemaphoreType.DMA((4,)),
            pltpu.SemaphoreType.DMA((2,)),
            pltpu.SemaphoreType.DMA((5, 4, 3)),
            pltpu.SemaphoreType.DMA((5, 4, 3)),
        ],
        compiler_params=pltpu.CompilerParams(collective_id=0, has_side_effects=True, vmem_limit_bytes=VMEM_LIMIT),
    )(lengths, tokens, table, short_filter, long_filter, queries)


def finish_kernel(mix_in, sum_hbm, mix_out, pool_out, mix_s, in_sem, out_sem, sum_s, pool_s, sum_sem, pool_sem):
    moves, copies, reads = [], [], []
    for n in range(8):
        rows = (n // 4, pl.ds(64 * (n % 4), 64))
        read = pltpu.make_async_copy(mix_in.at[rows], mix_s.at[rows], in_sem.at[n])
        reads.append((rows, read))
    for w in range(2):
        for p in range(4):
            load = pltpu.make_async_copy(sum_hbm.at[p, w], sum_s.at[p, w], sum_sem.at[p, w])
            load.start()
            moves.append(load)
    for rows, read in reads:
        read.start()
    for w in range(2):
        for p in range(4):
            moves[4 * w + p].wait()
            tiles = [sum_s[p, w, n].astype(f32) for n in range(32)]
            square = sum(t * t for t in tiles)
            mean = jnp.sum(square, axis=1, keepdims=True) * (1.0 / 4096)
            scale = 1.0 / jnp.sqrt(mean + 1e-06)
            for n in range(32):
                pool_s[w, 16 * p:16 * p + 16, 128 * n:128 * n + 128] = tiles[n] * scale
            rows = (w, pl.ds(16 * p, 16))
            copy = pltpu.make_async_copy(pool_s.at[rows], pool_out.at[rows], pool_sem.at[w, p])
            copy.start()
            copies.append(copy)
            rows, read = reads[4 * w + p]
            read.wait()
            copy = pltpu.make_async_copy(mix_s.at[rows], mix_out.at[rows], out_sem.at[4 * w + p])
            copy.start()
            copies.append(copy)
    for copy in copies:
        copy.wait()


def finish_call(mixed, summed):
    hbm = pl.BlockSpec(memory_space=pltpu.HBM)
    return pl.pallas_call(
        finish_kernel,
        in_specs=[hbm, hbm],
        out_specs=[hbm, hbm],
        out_shape=[jax.ShapeDtypeStruct((2, 256, 4096), bf16), jax.ShapeDtypeStruct((2, 64, 4096), f32)],
        scratch_shapes=[pltpu.VMEM((2, 256, 4096), bf16), pltpu.SemaphoreType.DMA((8,)), pltpu.SemaphoreType.DMA((8,)),
                        pltpu.VMEM((4, 2, 32, 16, 128), bf16), pltpu.VMEM((2, 64, 4096), f32),
                        pltpu.SemaphoreType.DMA((4, 2)), pltpu.SemaphoreType.DMA((2, 4))],
        compiler_params=pltpu.CompilerParams(vmem_limit_bytes=VMEM_LIMIT),
    )(mixed, summed.reshape(4, 2, 32, 16, 128))


def on_device(tokens, lengths, feature_table, short_filter, long_filter, queries):
    mixed, summed = layer_call(lengths, tokens, feature_table, short_filter, long_filter, queries)
    return finish_call(mixed, summed)


def solution(mesh):
    return jax.shard_map(
        on_device,
        mesh=mesh,
        in_specs=(P("batch", "ctx"), P("batch"), P(), P(), P(), P()),
        out_specs=(P("batch", "ctx", None), P("batch", None, None)),
        check_vma=False,
    )
```

time: 54.4 us -> 52.2 us (0.960)
  local copies, waits for them, and re-layouts: 3.19 us -> 0 us
  Pallas kernels: 50.3 us -> 51.4 us
    unnamed x10 -> x0, local copies, waits for them, and re-layouts: 1.62 us -> none
    slice x1 -> x0, local copies, waits for them, and re-layouts: 1.57 us -> none  [prep_call(): lax.slice(table, (64, 0), (128, 12288))]
    pallas_call x4 -> x2, Pallas kernels: 50.3 us -> 51.4 us  [the longest x1 46.5 us: layer_call(): pl.pallas_call(layer_kernel, in_specs=[pl.BlockSpec(memory_space=pltpu.SM...]
where the time goes in v3:
time: 52.2 us; the launch traced here: 52 us
  Pallas kernels  51.4 us (98%)
  between operations  0.64 us (1%)
    pallas_call x1, Pallas kernels, layer_call(): pl.pallas_call(layer_kernel, in_specs=[pl.BlockSpec(memory_space=pltpu.SM...  46.5 us
    pallas_call x1, Pallas kernels, finish_call(): pl.pallas_call(finish_kernel, in_specs=[hbm, hbm], out_specs=[hbm, hbm],...  4.92 us

profile of v3, /device:TPU:0, one launch (start us, length us, event | category | flops | bytes accessed | tf_op | source)
XLA Modules:
  0.0 52.0 jit_solution(8661293508373762534)
XLA Ops:
  0.6 46.5 %shard_map.77 = (bf16[2,256,4096]{2,1,0:T(8,128)(2,1)}, bf16[4,4,4,4,16,128]{5,4,3,2,1,0:T(8,128)(2,1)}) custom-call(s32[2]{0:T(128)} %len_ref.1, s32[2,256]{1,0:T(2,128)} %tok_hbm.1, bf16[512,12288]{1,0:T(8,128)(2,1)} %table_hbm.1, f32[3,12288]{1,0:T(4,128)} %sf_hbm.1, bf16[256,128]{1,0:T(8,128)(2,1)} %h_hbm.1, bf16[64,4096]{1,0:T(8,128)(2,1)} %qry_hbm.1), custom_call_target="tpu_custom_call" | custom-call | tf_op jit(solution)/shard_map/pallas_call | solution.py:258
  47.1 4.9 %shard_map.78 = (bf16[2,256,4096]{2,1,0:T(8,128)(2,1)}, f32[2,64,4096]{2,1,0:T(8,128)}) custom-call(bf16[2,256,4096]{2,1,0:T(8,128)(2,1)} %get-tuple-element.4.mix_in, bf16[4,2,32,16,128]{4,3,2,1,0:T(8,128)(2,1)} %bitcast.1), custom_call_target="tpu_custom_call" | custom-call | tf_op jit(solution)/shard_map/pallas_call | solution.py:333

commit v4 on v3

--- a/solution.py
+++ b/solution.py
@@ -17,7 +17,7 @@
 WIDE = 1024
 T = 128
 LOWEST = -1e38
-VMEM_LIMIT = 60 * 2**20
+VMEM_LIMIT = 54 * 2**20
 
 
 def build_tables(rows_s, sf_s, tab_s):
@@ -43,10 +43,8 @@
         mid = rest.astype(bf16).astype(f32)
         low = rest - mid
         stacked = jnp.concatenate([hi, mid, low, jnp.zeros((56, WIDE), f32)], axis=0).astype(bf16)
-        for u in range(WIDE // T):
-            turned = lax.dot_general(eye, stacked[:, T * u:T * u + T], (((1,), (1,)), ((), ())),
-                                     preferred_element_type=f32)
-            tab_s[pl.ds(base + T * u, T), :] = turned.astype(bf16)
+        for u in range(0, WIDE, T):
+            tab_s[pl.ds(base + u, T), :] = stacked[:, u:u + T].T
 
 
 def build_hot(prev, tok_s, oh_s):
@@ -93,9 +91,9 @@
     s_s[...] += dot(qry_s[step], m_s[pl.ds(base, CB), :])
 
 
-def layer_kernel(len_ref, tok_hbm, table_hbm, sf_hbm, h_hbm, qry_hbm, mix_out, sum_out,
-                 tok_s, prev_s, rows_s, sf_s, h_s, qry_s, tab_s, oh_s, g_s, q_s, m_ref, s_ref, mix_s,
-                 part_s, r1, s1f, s2, r2, r3, out_ref, load_sem, qry_sem, mix_sem, own_sem, tok_sem, send_sem, recv_sem):
+def layer_kernel(len_ref, tok_hbm, table_hbm, sf_hbm, h_hbm, qry_hbm, mix_s, out_ref,
+                 tok_s, prev_s, rows_s, sf_s, h_s, qry_s, tab_s, oh_s, g_s, q_s, m_ref, s_ref,
+                 part_s, r1, s1f, s2, r2, r3, load_sem, qry_sem, tok_sem, send_sem, recv_sem):
     me = lax.axis_index("ctx")
     core = lax.axis_index("batch")
     coord = [lax.rem(me // st, 4) for st in STRIDES]
@@ -136,11 +134,6 @@
     def _(step):
         mix_block(step, tab_s, oh_s, h_s, qry_s, g_s, q_s, m_ref, s_ref, mix_s)
 
-    writes = []
-    for n in range(STEPS):
-        write = pltpu.make_async_copy(mix_s.at[n], mix_out.at[:, :, pl.ds(CB * n, CB)], mix_sem.at[n])
-        write.start()
-        writes.append(write)
     lane = lax.broadcasted_iota(jnp.int32, (16, 128), 1)
 
     def top_tile(top):
@@ -239,27 +232,23 @@
             remote(spot, spot, 3, p, d, 1).wait_recv()
         spot = out_ref.at[p, mine[p][0]]
         for d in (2, 1, 3):
-            go(spot, sum_out.at[p, mine[p][0]], 4, p, d, 0)
-        keep = pltpu.make_async_copy(spot, sum_out.at[p, mine[p][0]], own_sem.at[p])
-        keep.start()
-        writes.append(keep)
-    for p in range(4):
-        for d in (1, 2, 3):
-            spot = sum_out.at[p, lax.rem(mine[p][0] + 4 - d, 4)]
+            go(spot, spot, 4, p, d, 0)
+    for p in range(4):
+        for d in (1, 2, 3):
+            spot = out_ref.at[p, lax.rem(mine[p][0] + 4 - d, 4)]
             remote(spot, spot, 4, p, d, 0).wait_recv()
     for copy in sends:
         copy.wait_send()
-    for write in writes:
-        write.wait()
 
 
 def layer_call(lengths, tokens, table, short_filter, long_filter, queries):
     hbm = pl.BlockSpec(memory_space=pltpu.HBM)
+    vmem = pl.BlockSpec(memory_space=pltpu.VMEM)
     return pl.pallas_call(
         layer_kernel,
         in_specs=[pl.BlockSpec(memory_space=pltpu.SMEM)] + [hbm] * 5,
-        out_specs=[hbm, hbm],
-        out_shape=[jax.ShapeDtypeStruct((2, 256, 4096), bf16), jax.ShapeDtypeStruct((4, 4, 4, 4, 16, 128), bf16)],
+        out_specs=[vmem, vmem],
+        out_shape=[pltpu.VMEM((STEPS, 2, 256, CB), bf16), pltpu.VMEM((4, 4, 4, 4, 16, 128), bf16)],
         scratch_shapes=[
             pltpu.VMEM((2, 256), jnp.int32),
             pltpu.VMEM((2, 256), jnp.int32),
@@ -273,18 +262,14 @@
             pltpu.VMEM((CB, 512), f32),
             pltpu.VMEM((4096, 512), bf16),
             pltpu.VMEM((64, 512), f32),
-            pltpu.VMEM((STEPS, 2, 256, CB), bf16),
             pltpu.VMEM((4, 4, 17, 16, 128), bf16),
             pltpu.VMEM((4, 3, 17, 16, 128), bf16),
             pltpu.VMEM((4, 4, 4, 16, 128), f32),
             pltpu.VMEM((4, 4, 5, 16, 128), bf16),
             pltpu.VMEM((4, 3, 5, 16, 128), bf16),
             pltpu.VMEM((4, 4, 5, 16, 128), bf16),
-            pltpu.VMEM((4, 4, 4, 4, 16, 128), bf16),
             pltpu.SemaphoreType.DMA((4,)),
             pltpu.SemaphoreType.DMA((STEPS,)),
-            pltpu.SemaphoreType.DMA((STEPS,)),
-            pltpu.SemaphoreType.DMA((4,)),
             pltpu.SemaphoreType.DMA((2,)),
             pltpu.SemaphoreType.DMA((5, 4, 3)),
             pltpu.SemaphoreType.DMA((5, 4, 3)),
@@ -293,22 +278,14 @@
     )(lengths, tokens, table, short_filter, long_filter, queries)
 
 
-def finish_kernel(mix_in, sum_hbm, mix_out, pool_out, mix_s, in_sem, out_sem, sum_s, pool_s, sum_sem, pool_sem):
-    moves, copies, reads = [], [], []
-    for n in range(8):
-        rows = (n // 4, pl.ds(64 * (n % 4), 64))
-        read = pltpu.make_async_copy(mix_in.at[rows], mix_s.at[rows], in_sem.at[n])
-        reads.append((rows, read))
+def finish_kernel(mix_s, sum_s, mix_out, pool_out, pool_s, mix_sem, pool_sem):
+    copies = []
+    for n in range(STEPS):
+        copy = pltpu.make_async_copy(mix_s.at[n], mix_out.at[:, :, pl.ds(CB * n, CB)], mix_sem.at[n])
+        copy.start()
+        copies.append(copy)
     for w in range(2):
         for p in range(4):
-            load = pltpu.make_async_copy(sum_hbm.at[p, w], sum_s.at[p, w], sum_sem.at[p, w])
-            load.start()
-            moves.append(load)
-    for rows, read in reads:
-        read.start()
-    for w in range(2):
-        for p in range(4):
-            moves[4 * w + p].wait()
             tiles = [sum_s[p, w, n].astype(f32) for n in range(32)]
             square = sum(t * t for t in tiles)
             mean = jnp.sum(square, axis=1, keepdims=True) * (1.0 / 4096)
@@ -319,26 +296,20 @@
             copy = pltpu.make_async_copy(pool_s.at[rows], pool_out.at[rows], pool_sem.at[w, p])
             copy.start()
             copies.append(copy)
-            rows, read = reads[4 * w + p]
-            read.wait()
-            copy = pltpu.make_async_copy(mix_s.at[rows], mix_out.at[rows], out_sem.at[4 * w + p])
-            copy.start()
-            copies.append(copy)
     for copy in copies:
         copy.wait()
 
 
 def finish_call(mixed, summed):
     hbm = pl.BlockSpec(memory_space=pltpu.HBM)
+    vmem = pl.BlockSpec(memory_space=pltpu.VMEM)
     return pl.pallas_call(
         finish_kernel,
-        in_specs=[hbm, hbm],
+        in_specs=[vmem, vmem],
         out_specs=[hbm, hbm],
         out_shape=[jax.ShapeDtypeStruct((2, 256, 4096), bf16), jax.ShapeDtypeStruct((2, 64, 4096), f32)],
-        scratch_shapes=[pltpu.VMEM((2, 256, 4096), bf16), pltpu.SemaphoreType.DMA((8,)), pltpu.SemaphoreType.DMA((8,)),
-                        pltpu.VMEM((4, 2, 32, 16, 128), bf16), pltpu.VMEM((2, 64, 4096), f32),
-                        pltpu.SemaphoreType.DMA((4, 2)), pltpu.SemaphoreType.DMA((2, 4))],
-        compiler_params=pltpu.CompilerParams(vmem_limit_bytes=VMEM_LIMIT),
+        scratch_shapes=[pltpu.VMEM((2, 64, 4096), f32), pltpu.SemaphoreType.DMA((STEPS,)), pltpu.SemaphoreType.DMA((2, 4))],
+        compiler_params=pltpu.CompilerParams(vmem_limit_bytes=16 * 2**20),
     )(mixed, summed.reshape(4, 2, 32, 16, 128))
 
 

time: 52.2 us -> 49.6 us (0.950)
  Pallas kernels: 51.4 us -> 48.8 us
    pallas_call x1, Pallas kernels: 4.92 us -> 2.89 us  [finish_call(): pl.pallas_call(finish_kernel, in_specs=[vmem, vmem], out_specs=[hbm, hbm]...]
    pallas_call x1, Pallas kernels: 46.5 us -> 45.9 us  [layer_call(): pl.pallas_call(layer_kernel, in_specs=[pl.BlockSpec(memory_space=pltpu.SM...]
where the time goes in v4:
time: 49.6 us; the launch traced here: 49.5 us
  Pallas kernels  48.8 us (98%)
  between operations  0.64 us (1%)
    pallas_call x1, Pallas kernels, layer_call(): pl.pallas_call(layer_kernel, in_specs=[pl.BlockSpec(memory_space=pltpu.SM...  45.9 us
    pallas_call x1, Pallas kernels, finish_call(): pl.pallas_call(finish_kernel, in_specs=[vmem, vmem], out_specs=[hbm, hbm]...  2.89 us

profile of v4, /device:TPU:0, one launch (start us, length us, event | category | flops | bytes accessed | tf_op | source)
XLA Modules:
  0.0 49.5 jit_solution(13325780012925513428)
XLA Ops:
  0.6 45.9 %shard_map.77 = (bf16[4,2,256,1024]{3,2,1,0:T(8,128)(2,1)S(1)}, bf16[4,4,4,4,16,128]{5,4,3,2,1,0:T(8,128)(2,1)S(1)}) custom-call(s32[2]{0:T(128)} %len_ref.1, s32[2,256]{1,0:T(2,128)} %tok_hbm.1, bf16[512,12288]{1,0:T(8,128)(2,1)} %table_hbm.1, f32[3,12288]{1,0:T(4,128)} %sf_hbm.1, bf16[256,128]{1,0:T(8,128)(2,1)} %h_hbm.1, bf16[64,4096]{1,0:T(8,128)(2,1)} %qry_hbm.1), custom_call_target="tpu_custom_call" | custom-call | tf_op jit(solution)/shard_map/pallas_call | solution.py:247
  46.6 2.9 %shard_map.78 = (bf16[2,256,4096]{2,1,0:T(8,128)(2,1)}, f32[2,64,4096]{2,1,0:T(8,128)}) custom-call(bf16[4,2,256,1024]{3,2,1,0:T(8,128)(2,1)S(1)} %get-tuple-element.4.mix_s, bf16[4,2,32,16,128]{4,3,2,1,0:T(8,128)(2,1)S(1)} %bitcast.1), custom_call_target="tpu_custom_call" | custom-call | tf_op jit(solution)/shard_map/pallas_call | solution.py:306

commit v5 on v4

--- a/solution.py
+++ b/solution.py
@@ -100,7 +100,7 @@
     peer = [[me + (lax.rem(coord[a] + d, 4) - coord[a]) * STRIDES[a] for d in range(4)] for a in range(3)]
 
     def mixed(values, p, stage):
-        first, second = values[(p + stage) % 3], values[(p + stage + 1) % 3]
+        first, second = values[(p + stage) % 3], values[(p + stage + 2) % 3]
         return first + core * (second - first)
 
     mine = [[mixed(coord, p, s) for s in range(3)] for p in range(4)]

time: 49.6 us -> 48.9 us (0.986)
  Pallas kernels: 48.8 us -> 48.1 us
    pallas_call x1, Pallas kernels: 45.9 us -> 45.2 us  [layer_call(): pl.pallas_call(layer_kernel, in_specs=[pl.BlockSpec(memory_space=pltpu.SM...]
where the time goes in v5:
time: 48.9 us; the launch traced here: 48.7 us
  Pallas kernels  48.1 us (98%)
  between operations  0.64 us (1%)
    pallas_call x1, Pallas kernels, layer_call(): pl.pallas_call(layer_kernel, in_specs=[pl.BlockSpec(memory_space=pltpu.SM...  45.2 us
    pallas_call x1, Pallas kernels, finish_call(): pl.pallas_call(finish_kernel, in_specs=[vmem, vmem], out_specs=[hbm, hbm]...  2.89 us

profile of v5, /device:TPU:0, one launch (start us, length us, event | category | flops | bytes accessed | tf_op | source)
XLA Modules:
  0.0 48.7 jit_solution(11692892366730711266)
XLA Ops:
  0.6 45.2 %shard_map.77 = (bf16[4,2,256,1024]{3,2,1,0:T(8,128)(2,1)S(1)}, bf16[4,4,4,4,16,128]{5,4,3,2,1,0:T(8,128)(2,1)S(1)}) custom-call(s32[2]{0:T(128)} %len_ref.1, s32[2,256]{1,0:T(2,128)} %tok_hbm.1, bf16[512,12288]{1,0:T(8,128)(2,1)} %table_hbm.1, f32[3,12288]{1,0:T(4,128)} %sf_hbm.1, bf16[256,128]{1,0:T(8,128)(2,1)} %h_hbm.1, bf16[64,4096]{1,0:T(8,128)(2,1)} %qry_hbm.1), custom_call_target="tpu_custom_call" | custom-call | tf_op jit(solution)/shard_map/pallas_call | solution.py:247
  45.9 2.9 %shard_map.78 = (bf16[2,256,4096]{2,1,0:T(8,128)(2,1)}, f32[2,64,4096]{2,1,0:T(8,128)}) custom-call(bf16[4,2,256,1024]{3,2,1,0:T(8,128)(2,1)S(1)} %get-tuple-element.4.mix_s, bf16[4,2,32,16,128]{4,3,2,1,0:T(8,128)(2,1)S(1)} %bitcast.1), custom_call_target="tpu_custom_call" | custom-call | tf_op jit(solution)/shard_map/pallas_call | solution.py:306

commit v6 on v5

--- a/solution.py
+++ b/solution.py
@@ -14,7 +14,7 @@
 CB = 1024
 STEPS = 4096 // CB
 UNIT = 256
-WIDE = 1024
+WIDE = 2048
 T = 128
 LOWEST = -1e38
 VMEM_LIMIT = 54 * 2**20

time: 48.9 us -> 48.7 us (level)
  no operation moved by 1% of the time
where the time goes in v6:
time: 48.7 us; the launch traced here: 48.6 us
  Pallas kernels  47.9 us (98%)
  between operations  0.64 us (1%)
    pallas_call x1, Pallas kernels, layer_call(): pl.pallas_call(layer_kernel, in_specs=[pl.BlockSpec(memory_space=pltpu.SM...  45 us
    pallas_call x1, Pallas kernels, finish_call(): pl.pallas_call(finish_kernel, in_specs=[vmem, vmem], out_specs=[hbm, hbm]...  2.89 us

profile of v6, /device:TPU:0, one launch (start us, length us, event | category | flops | bytes accessed | tf_op | source)
XLA Modules:
  0.0 48.6 jit_solution(15720920251293282300)
XLA Ops:
  0.6 45.0 %shard_map.77 = (bf16[4,2,256,1024]{3,2,1,0:T(8,128)(2,1)S(1)}, bf16[4,4,4,4,16,128]{5,4,3,2,1,0:T(8,128)(2,1)S(1)}) custom-call(s32[2]{0:T(128)} %len_ref.1, s32[2,256]{1,0:T(2,128)} %tok_hbm.1, bf16[512,12288]{1,0:T(8,128)(2,1)} %table_hbm.1, f32[3,12288]{1,0:T(4,128)} %sf_hbm.1, bf16[256,128]{1,0:T(8,128)(2,1)} %h_hbm.1, bf16[64,4096]{1,0:T(8,128)(2,1)} %qry_hbm.1), custom_call_target="tpu_custom_call" | custom-call | tf_op jit(solution)/shard_map/pallas_call | solution.py:247
  45.7 2.9 %shard_map.78 = (bf16[2,256,4096]{2,1,0:T(8,128)(2,1)}, f32[2,64,4096]{2,1,0:T(8,128)}) custom-call(bf16[4,2,256,1024]{3,2,1,0:T(8,128)(2,1)S(1)} %get-tuple-element.4.mix_s, bf16[4,2,32,16,128]{4,3,2,1,0:T(8,128)(2,1)S(1)} %bitcast.1), custom_call_target="tpu_custom_call" | custom-call | tf_op jit(solution)/shard_map/pallas_call | solution.py:306

commit v7 on v6

--- a/solution.py
+++ b/solution.py
@@ -60,7 +60,7 @@
         oh_s[:, 256 + 256 * w:512 + 256 * w] = full[:, 128:]
 
 
-def mix_block(step, tab_s, oh_s, h_s, qry_s, g_s, q_s, m_s, s_s, mix_s):
+def mix_block(step, tab_s, oh_s, h_s, qry_s, g_s, q_s, m_s, s_s):
     dot = functools.partial(jnp.dot, preferred_element_type=f32)
     s_i = lax.broadcasted_iota(jnp.int32, (T, T), 0)
     t_i = lax.broadcasted_iota(jnp.int32, (T, T), 1)
@@ -83,12 +83,15 @@
         conv = dot(lhs, toep)
         conv = jnp.concatenate([conv[16 * b:16 * b + 16] for b in range(4)], axis=1)
         m_s[pl.ds(base + 16 * j, 16), :] = (q_s[rows, :] * conv).astype(bf16)
+    s_s[...] += dot(qry_s[step], m_s[pl.ds(base, CB), :])
+
+
+def turn_block(step, m_s, mix_s):
+    base = pl.multiple_of(step * CB, CB)
     for u in range(CB // UNIT):
-        rows = pl.ds(base + UNIT * u, UNIT)
-        m = m_s[rows, :]
+        m = m_s[pl.ds(base + UNIT * u, UNIT), :]
         for w in range(2):
             mix_s[step, w, :, UNIT * u:UNIT * u + UNIT] = m[:, 256 * w:256 * w + 256].T
-    s_s[...] += dot(qry_s[step], m_s[pl.ds(base, CB), :])
 
 
 def layer_kernel(len_ref, tok_hbm, table_hbm, sf_hbm, h_hbm, qry_hbm, mix_s, out_ref,
@@ -132,7 +135,7 @@
 
     @pl.loop(0, STEPS)
     def _(step):
-        mix_block(step, tab_s, oh_s, h_s, qry_s, g_s, q_s, m_ref, s_ref, mix_s)
+        mix_block(step, tab_s, oh_s, h_s, qry_s, g_s, q_s, m_ref, s_ref)
 
     lane = lax.broadcasted_iota(jnp.int32, (16, 128), 1)
 
@@ -175,6 +178,10 @@
     for p in range(4):
         for d in (2, 1, 3):
             go(part_s.at[lax.rem(mine[p][0] + d, 4), p], r1.at[p, d - 1], 0, p, d, 0)
+
+    @pl.loop(0, STEPS)
+    def _(step):
+        turn_block(step, m_ref, mix_s)
 
     def read_top(tile):
         return jnp.sum(tile.astype(f32), axis=1, keepdims=True)

time: 48.7 us -> 48.3 us (level)
  no operation moved by 1% of the time
where the time goes in v7:
time: 48.3 us; the launch traced here: 48.2 us
  Pallas kernels  47.5 us (98%)
  between operations  0.64 us (1%)
    pallas_call x1, Pallas kernels, layer_call(): pl.pallas_call(layer_kernel, in_specs=[pl.BlockSpec(memory_space=pltpu.SM...  44.7 us
    pallas_call x1, Pallas kernels, finish_call(): pl.pallas_call(finish_kernel, in_specs=[vmem, vmem], out_specs=[hbm, hbm]...  2.89 us

profile of v7, /device:TPU:0, one launch (start us, length us, event | category | flops | bytes accessed | tf_op | source)
XLA Modules:
  0.0 48.2 jit_solution(6820652407202861961)
XLA Ops:
  0.6 44.7 %shard_map.77 = (bf16[4,2,256,1024]{3,2,1,0:T(8,128)(2,1)S(1)}, bf16[4,4,4,4,16,128]{5,4,3,2,1,0:T(8,128)(2,1)S(1)}) custom-call(s32[2]{0:T(128)} %len_ref.1, s32[2,256]{1,0:T(2,128)} %tok_hbm.1, bf16[512,12288]{1,0:T(8,128)(2,1)} %table_hbm.1, f32[3,12288]{1,0:T(4,128)} %sf_hbm.1, bf16[256,128]{1,0:T(8,128)(2,1)} %h_hbm.1, bf16[64,4096]{1,0:T(8,128)(2,1)} %qry_hbm.1), custom_call_target="tpu_custom_call" | custom-call | tf_op jit(solution)/shard_map/pallas_call | solution.py:254
  45.3 2.9 %shard_map.78 = (bf16[2,256,4096]{2,1,0:T(8,128)(2,1)}, f32[2,64,4096]{2,1,0:T(8,128)}) custom-call(bf16[4,2,256,1024]{3,2,1,0:T(8,128)(2,1)S(1)} %get-tuple-element.4.mix_s, bf16[4,2,32,16,128]{4,3,2,1,0:T(8,128)(2,1)S(1)} %bitcast.1), custom_call_target="tpu_custom_call" | custom-call | tf_op jit(solution)/shard_map/pallas_call | solution.py:313
